TPU v7x, 32 devices: a whole 2x2x4 slice. The times are simulated.
32 devices in a mesh: dp: 8 (over z, x), tensor: 4 (over y, core).
Axes of the slice: x: 2, y: 2, z: 4, core: 2. Of those that a mesh axis runs over, the one named last changes fastest.
Arguments:
- inputs: bfloat16 [32, 196, 768], P('dp'), may hold values from -6 to 6
- target: bfloat16 [32, 196, 768], P('dp'), may hold values from -6 to 6
- valid: int32 [32, 196], P('dp'), may hold values from 0 to 1, as said below
- first_gain: float32 [768], replicated, may hold values from 0.5 to 1.5
- first_shift: float32 [768], replicated, may hold values from -3 to 3
- triple_weight: bfloat16 [3, 768, 768], P(None, 'dp', 'tensor'), may hold values from -0.21875 to 0.21875
- query_value_bias: float32 [2, 768], P(None, 'tensor'), may hold values from -3 to 3
- output_weight: bfloat16 [768, 768], P('tensor', 'dp'), may hold values from -0.875 to 0.875
- output_bias: float32 [768], replicated, may hold values from -3 to 3
- second_gain: float32 [768], replicated, may hold values from 0.5 to 1.5
- second_shift: float32 [768], replicated, may hold values from -3 to 3
- expand_weight: bfloat16 [768, 3072], P('dp', 'tensor'), may hold values from -0.21875 to 0.21875
- expand_bias: float32 [3072], P('tensor'), may hold values from -3 to 3
- shrink_weight: bfloat16 [3072, 768], P('tensor', 'dp'), may hold values from -0.109375 to 0.109375
- shrink_bias: float32 [768], replicated, may hold values from -3 to 3
- rows_table: float32 [27, 64], replicated, may hold values from -0.6 to 0.6
- columns_table: float32 [27, 64], replicated, may hold values from -0.6 to 0.6
Outputs:
- block_output: bfloat16 [32, 196, 768], P('dp')
- loss: float32 [], replicated
- input_grad: float32 [32, 196, 768], P('dp')
- first_gain_grad: float32 [768], replicated
- first_shift_grad: float32 [768], replicated
- triple_weight_grad: float32 [3, 768, 768], P(None, 'dp', 'tensor')
- query_value_bias_grad: float32 [2, 768], P(None, 'tensor')
- output_weight_grad: float32 [768, 768], P('tensor', 'dp')
- output_bias_grad: float32 [768], replicated
- second_gain_grad: float32 [768], replicated
- second_shift_grad: float32 [768], replicated
- expand_weight_grad: float32 [768, 3072], P('dp', 'tensor')
- expand_bias_grad: float32 [3072], P('tensor')
- shrink_weight_grad: float32 [3072, 768], P('tensor', 'dp')
- shrink_bias_grad: float32 [768], replicated
- rows_table_grad: float32 [27, 64], replicated
- columns_table_grad: float32 [27, 64], replicated
Inputs may be any that keep to these rules, and one draw needn't show every extreme that they name: `valid`: 1 marks an image token and 0 a padding token; the image tokens of a window fill a rectangle of its first rows and first columns, and every window holds at least one.
All inputs are finite; a program needn't handle non-finite values.
Results may differ from a plain program's by a relative error of at most 0.012.
Values may be sent and summed in bfloat16 or wider, within the bound.
A program may use at most 128 MiB of HBM per device.

v0:
```python
import math

import jax
import jax.numpy as jnp
from jax import lax
from jax.sharding import PartitionSpec as P

D = 768
HEADS = 12
HEAD = 64
WIN = 14
WIN_TOK = 196
MICRO = 2


def normalize(values):
    center = jnp.mean(values, axis=-1, keepdims=True)
    centered = values - center
    spread = jnp.mean(centered * centered, axis=-1, keepdims=True)
    inverse = lax.rsqrt(spread + 1e-06)
    return (centered * inverse, inverse)


def normalize_back(grad_out, unit, inverse, gain):
    scaled = grad_out * gain
    mean_one = jnp.mean(scaled, axis=-1, keepdims=True)
    mean_two = jnp.mean(scaled * unit, axis=-1, keepdims=True)
    return inverse * (scaled - mean_one - unit * mean_two)


def position_select(side):
    shape = (side, side, 2 * side - 1)
    first = lax.broadcasted_iota(jnp.int32, shape, 0)
    second = lax.broadcasted_iota(jnp.int32, shape, 1)
    slots = lax.broadcasted_iota(jnp.int32, shape, 2)
    return (slots == first - second + side - 1).astype(jnp.bfloat16)


def score_block(queries, keys, table_rows, table_cols, scale_factor):
    groups = queries.shape[0]
    side = queries.shape[1]
    heads = queries.shape[3]
    along_rows = jnp.einsum(
        "gabnc,aec->gnabe", queries, table_rows, preferred_element_type=jnp.float32
    )
    along_cols = jnp.einsum(
        "gabnc,bfc->gnabf", queries, table_cols, preferred_element_type=jnp.float32
    )
    scores = (
        jnp.einsum("gabnc,gefnc->gnabef", queries, keys, preferred_element_type=jnp.float32)
        * scale_factor
    )
    scores = scores + along_rows[..., :, None] + along_cols[..., None, :]
    return scores.reshape(groups, heads, side * side, side * side)


def gelu_exact(inner):
    return jax.nn.gelu(inner, approximate=False)


def row_total(partial_value):
    return lax.psum(partial_value, "tensor")


def share_of(values):
    share_rows = values.shape[0] // lax.axis_size("tensor")
    return lax.dynamic_slice_in_dim(values, lax.axis_index("tensor") * share_rows, share_rows, 0)


def shards(
    inputs,
    target,
    valid,
    first_gain,
    first_shift,
    triple_weight,
    query_value_bias,
    output_weight,
    output_bias,
    second_gain,
    second_shift,
    expand_weight,
    expand_bias,
    shrink_weight,
    shrink_bias,
    rows_table,
    columns_table,
):
    local_heads = HEADS // lax.axis_size("tensor")
    local_width = local_heads * HEAD
    local_windows = inputs.shape[0]
    win_micro = local_windows // MICRO
    micro_rows = win_micro * WIN_TOK
    scale_factor = 1.0 / math.sqrt(HEAD)
    highest = lax.Precision.HIGHEST
    live = valid.astype(jnp.float32)
    select = position_select(WIN)
    table_rows = jnp.einsum(
        "aej,jc->aec", select, rows_table.astype(jnp.bfloat16), preferred_element_type=jnp.float32
    ).astype(jnp.bfloat16)
    table_cols = jnp.einsum(
        "aej,jc->aec",
        select,
        columns_table.astype(jnp.bfloat16),
        preferred_element_type=jnp.float32,
    ).astype(jnp.bfloat16)
    rows_float = table_rows.astype(jnp.float32)
    cols_float = table_cols.astype(jnp.float32)
    triple_bias = jnp.stack(
        [query_value_bias[0], jnp.zeros_like(query_value_bias[0]), query_value_bias[1]]
    )
    saved = []
    outputs = []
    local_loss = jnp.zeros((), jnp.float32)
    for micro in range(MICRO):
        gathered = (
            lax.all_gather(triple_weight, "dp", axis=1, tiled=True),
            lax.all_gather(output_weight, "dp", axis=1, tiled=True),
            lax.all_gather(expand_weight, "dp", axis=0, tiled=True),
            lax.all_gather(shrink_weight, "dp", axis=1, tiled=True),
        )
        full_triple, full_output, full_expand, full_shrink = gathered
        lower = micro * win_micro
        flat_rows = inputs[lower : lower + win_micro].reshape(micro_rows, D).astype(jnp.float32)
        unit_one, inverse_one = normalize(flat_rows)
        normed = (unit_one * first_gain + first_shift).astype(jnp.bfloat16)
        projected = (
            jnp.einsum("rd,tde->rte", normed, full_triple, preferred_element_type=jnp.float32)
            + triple_bias
        )
        projected = projected.astype(jnp.bfloat16)
        split = projected.reshape(win_micro, WIN, WIN, 3, local_heads, HEAD)
        queries = split[:, :, :, 0]
        keys = split[:, :, :, 1]
        values = split[:, :, :, 2].reshape(win_micro, WIN_TOK, local_heads, HEAD)
        scores = score_block(queries, keys, table_rows, table_cols, scale_factor)
        peak = jnp.max(scores, axis=-1, keepdims=True)
        raised = jnp.exp(scores - peak)
        denominator = jnp.sum(raised, axis=-1, keepdims=True)
        log_total = peak + jnp.log(denominator)
        softmaxed = (raised / denominator).astype(jnp.bfloat16)
        mixed = jnp.einsum("gnqk,gknc->gqnc", softmaxed, values, preferred_element_type=jnp.float32)
        mixed = mixed.reshape(micro_rows, local_width).astype(jnp.bfloat16)
        partial_attended = jnp.dot(mixed, full_output, preferred_element_type=jnp.float32)
        middle = flat_rows + (row_total(partial_attended) + output_bias)
        unit_two, inverse_two = normalize(middle)
        normed_two = (unit_two * second_gain + second_shift).astype(jnp.bfloat16)
        before = jnp.dot(normed_two, full_expand, preferred_element_type=jnp.float32) + expand_bias
        hidden = gelu_exact(before).astype(jnp.bfloat16)
        partial_shrunk = jnp.dot(hidden, full_shrink, preferred_element_type=jnp.float32)
        result = middle + (row_total(partial_shrunk) + shrink_bias)
        aim = target[lower : lower + win_micro].reshape(micro_rows, D).astype(jnp.float32)
        marks = live[lower : lower + win_micro].reshape(micro_rows, 1)
        weighted_gap = marks * (result - aim)
        local_loss = local_loss + jnp.sum(weighted_gap * (result - aim))
        outputs.append(result.astype(jnp.bfloat16).reshape(win_micro, WIN_TOK, D))
        saved.append(
            (
                unit_one,
                inverse_one,
                normed,
                projected,
                log_total,
                mixed,
                unit_two,
                inverse_two,
                normed_two,
                before,
                hidden,
                weighted_gap,
            )
        )
    loss_total, count = lax.psum((local_loss, jnp.sum(live)), "dp")
    loss = loss_total / (count * D)
    grad_scale = local_windows * WIN_TOK * lax.axis_size("dp") / count
    triple_acc = jnp.zeros((3, D, local_width), jnp.float32)
    output_acc = jnp.zeros((local_width, D), jnp.float32)
    expand_acc = jnp.zeros((D, full_expand.shape[1]), jnp.float32)
    shrink_acc = jnp.zeros((full_shrink.shape[0], D), jnp.float32)
    first_gain_acc = jnp.zeros((D,), jnp.float32)
    first_shift_acc = jnp.zeros((D,), jnp.float32)
    second_gain_acc = jnp.zeros((D,), jnp.float32)
    second_shift_acc = jnp.zeros((D,), jnp.float32)
    output_bias_acc = jnp.zeros((D,), jnp.float32)
    shrink_bias_acc = jnp.zeros((D,), jnp.float32)
    expand_bias_acc = jnp.zeros((full_expand.shape[1],), jnp.float32)
    query_value_acc = jnp.zeros((2, local_width), jnp.float32)
    rows_expanded_acc = jnp.zeros((WIN, WIN, HEAD), jnp.float32)
    cols_expanded_acc = jnp.zeros((WIN, WIN, HEAD), jnp.float32)
    input_grads = []
    for micro in range(MICRO):
        gathered = (
            lax.all_gather(triple_weight, "dp", axis=1, tiled=True),
            lax.all_gather(output_weight, "dp", axis=1, tiled=True),
            lax.all_gather(expand_weight, "dp", axis=0, tiled=True),
            lax.all_gather(shrink_weight, "dp", axis=1, tiled=True),
        )
        full_triple, full_output, full_expand, full_shrink = gathered
        (
            unit_one,
            inverse_one,
            normed,
            projected,
            log_total,
            mixed,
            unit_two,
            inverse_two,
            normed_two,
            before,
            hidden,
            weighted_gap,
        ) = saved[micro]
        grad_result = grad_scale * weighted_gap
        shrink_bias_acc = shrink_bias_acc + jnp.sum(share_of(grad_result), axis=0)
        grad_result_low = grad_result.astype(jnp.bfloat16)
        shrink_acc = shrink_acc + jnp.einsum(
            "rf,rd->fd", hidden, grad_result_low, preferred_element_type=jnp.float32
        )
        grad_hidden = jnp.einsum(
            "rd,fd->rf", grad_result_low, full_shrink, preferred_element_type=jnp.float32
        )
        unused, gelu_pull = jax.vjp(gelu_exact, before)
        grad_before = gelu_pull(grad_hidden)[0].astype(jnp.bfloat16)
        expand_bias_acc = expand_bias_acc + jnp.sum(grad_before.astype(jnp.float32), axis=0)
        expand_acc = expand_acc + jnp.einsum(
            "rd,rf->df", normed_two, grad_before, preferred_element_type=jnp.float32
        )
        partial_two = jnp.einsum(
            "rf,df->rd", grad_before, full_expand, preferred_element_type=jnp.float32
        )
        grad_normed_two = row_total(partial_two)
        grad_middle = grad_result + normalize_back(
            grad_normed_two, unit_two, inverse_two, second_gain
        )
        second_gain_acc = second_gain_acc + jnp.sum(share_of(grad_normed_two * unit_two), axis=0)
        second_shift_acc = second_shift_acc + jnp.sum(share_of(grad_normed_two), axis=0)
        output_bias_acc = output_bias_acc + jnp.sum(share_of(grad_middle), axis=0)
        grad_middle_low = grad_middle.astype(jnp.bfloat16)
        output_acc = output_acc + jnp.einsum(
            "rc,rd->cd", mixed, grad_middle_low, preferred_element_type=jnp.float32
        )
        grad_mixed = jnp.einsum(
            "rd,cd->rc", grad_middle_low, full_output, preferred_element_type=jnp.float32
        )
        grad_mixed = grad_mixed.astype(jnp.bfloat16).reshape(win_micro, WIN_TOK, local_heads, HEAD)
        split = projected.reshape(win_micro, WIN, WIN, 3, local_heads, HEAD)
        queries = split[:, :, :, 0]
        keys = split[:, :, :, 1]
        queries_flat = queries.reshape(win_micro, WIN_TOK, local_heads, HEAD)
        keys_flat = keys.reshape(win_micro, WIN_TOK, local_heads, HEAD)
        values = split[:, :, :, 2].reshape(win_micro, WIN_TOK, local_heads, HEAD)
        scores = score_block(queries, keys, table_rows, table_cols, scale_factor)
        softmax_exact = jnp.exp(scores - log_total)
        grad_soft = jnp.einsum(
            "gqnc,gknc->gnqk", grad_mixed, values, preferred_element_type=jnp.float32
        )
        delta = jnp.sum(softmax_exact * grad_soft, axis=-1, keepdims=True)
        grad_scores = (softmax_exact * (grad_soft - delta)).astype(jnp.bfloat16)
        grad_values = jnp.einsum(
            "gnqk,gqnc->gknc",
            softmax_exact.astype(jnp.bfloat16),
            grad_mixed,
            preferred_element_type=jnp.float32,
        )
        grad_keys = (
            jnp.einsum(
                "gnqk,gqnc->gknc", grad_scores, queries_flat, preferred_element_type=jnp.float32
            )
            * scale_factor
        )
        grad_queries = (
            jnp.einsum(
                "gnqk,gknc->gqnc", grad_scores, keys_flat, preferred_element_type=jnp.float32
            )
            * scale_factor
        )
        grad_grid = grad_scores.astype(jnp.float32).reshape(
            win_micro, local_heads, WIN, WIN, WIN, WIN
        )
        row_part = jnp.sum(grad_grid, axis=5)
        col_part = jnp.sum(grad_grid, axis=4)
        queries_float = queries.astype(jnp.float32)
        rel_queries = jnp.einsum("gnabe,aec->gabnc", row_part, rows_float, precision=highest)
        rel_queries = rel_queries + jnp.einsum(
            "gnabf,bfc->gabnc", col_part, cols_float, precision=highest
        )
        grad_queries = grad_queries + rel_queries.reshape(win_micro, WIN_TOK, local_heads, HEAD)
        rows_expanded_acc = rows_expanded_acc + jnp.einsum(
            "gnabe,gabnc->aec", row_part, queries_float, precision=highest
        )
        cols_expanded_acc = cols_expanded_acc + jnp.einsum(
            "gnabf,gabnc->bfc", col_part, queries_float, precision=highest
        )
        grad_projected = jnp.stack(
            [
                grad_queries.reshape(micro_rows, local_width),
                grad_keys.reshape(micro_rows, local_width),
                grad_values.reshape(micro_rows, local_width),
            ],
            axis=1,
        ).astype(jnp.bfloat16)
        projected_float_sums = jnp.sum(grad_projected.astype(jnp.float32), axis=0)
        query_value_acc = query_value_acc + jnp.stack(
            [projected_float_sums[0], projected_float_sums[2]]
        )
        triple_acc = triple_acc + jnp.einsum(
            "rd,rte->tde", normed, grad_projected, preferred_element_type=jnp.float32
        )
        partial_one = jnp.einsum(
            "rte,tde->rd", grad_projected, full_triple, preferred_element_type=jnp.float32
        )
        grad_normed = row_total(partial_one)
        grad_tokens = grad_middle + normalize_back(grad_normed, unit_one, inverse_one, first_gain)
        first_gain_acc = first_gain_acc + jnp.sum(share_of(grad_normed * unit_one), axis=0)
        first_shift_acc = first_shift_acc + jnp.sum(share_of(grad_normed), axis=0)
        input_grads.append(grad_tokens.reshape(win_micro, WIN_TOK, D))
    select_float = select.astype(jnp.float32)
    rows_table_part = jnp.einsum("aej,aec->jc", select_float, rows_expanded_acc, precision=highest)
    cols_table_part = jnp.einsum("aej,aec->jc", select_float, cols_expanded_acc, precision=highest)
    triple_grad, output_grad, expand_grad, shrink_grad = (
        lax.psum_scatter(triple_acc, "dp", scatter_dimension=1, tiled=True),
        lax.psum_scatter(output_acc, "dp", scatter_dimension=1, tiled=True),
        lax.psum_scatter(expand_acc, "dp", scatter_dimension=0, tiled=True),
        lax.psum_scatter(shrink_acc, "dp", scatter_dimension=1, tiled=True),
    )
    over_heads = lax.psum(
        (
            rows_table_part,
            cols_table_part,
            first_gain_acc,
            first_shift_acc,
            output_bias_acc,
            second_gain_acc,
            second_shift_acc,
            shrink_bias_acc,
        ),
        "tensor",
    )
    summed_small = lax.psum(
        (
            over_heads[0],
            over_heads[1],
            over_heads[2],
            over_heads[3],
            over_heads[4],
            over_heads[5],
            over_heads[6],
            over_heads[7],
            query_value_acc,
            expand_bias_acc,
        ),
        "dp",
    )
    return (
        jnp.concatenate(outputs, axis=0),
        loss,
        jnp.concatenate(input_grads, axis=0),
        summed_small[2],
        summed_small[3],
        triple_grad,
        summed_small[8],
        output_grad,
        summed_small[4],
        summed_small[5],
        summed_small[6],
        expand_grad,
        summed_small[9],
        shrink_grad,
        summed_small[7],
        summed_small[0],
        summed_small[1],
    )


def solution(mesh):
    placed = (
        P("dp", None, None),
        P("dp", None, None),
        P("dp", None),
        P(),
        P(),
        P(None, "dp", "tensor"),
        P(None, "tensor"),
        P("tensor", "dp"),
        P(),
        P(),
        P(),
        P("dp", "tensor"),
        P("tensor"),
        P("tensor", "dp"),
        P(),
        P(),
        P(),
    )
    return jax.shard_map(
        shards,
        mesh=mesh,
        in_specs=placed,
        out_specs=(
            P("dp", None, None),
            P(),
            P("dp", None, None),
            P(),
            P(),
            P(None, "dp", "tensor"),
            P(None, "tensor"),
            P("tensor", "dp"),
            P(),
            P(),
            P(),
            P("dp", "tensor"),
            P("tensor"),
            P("tensor", "dp"),
            P(),
            P(),
            P(),
        ),
        check_vma=False,
    )
```

profile of v0, /device:TPU:0, one launch (start us, length us, event | category | flops | bytes accessed | tf_op | source)
XLA Modules:
  0.0 731.7 jit_solution(15941391313740477688)
XLA Ops:
  17.2 39.1 %all_gather.8 = bf16[3,768,192]{2,0,1:T(4,128)(2,1)S(1)} all-gather(bf16[3,96,192]{2,0,1:T(4,128)(2,1)S(1)} %copy.259), channel_id=1, replica_groups=mesh['dp'=8,'tensor'=4] {'dp'}, dimensions={1}, use_global_device_ids=true | all-gather | bytes 995328 | tf_op jit(solution)/shard_map/all_gather | solution.py:117
  78.8 7.4 %fusion.122 = (f32[2,3,14,14]{3,2,1,0:T(8,128)S(1)}, f32[2,3,14,14,14,14]{3,5,4,2,1,0:T(8,128)}) fusion(f32[2,3,14,14,14]{3,4,2,1,0:T(8,128)} %copy.289, bf16[2,14,14,1,3,64]{5,4,2,1,0,3:T(4,128)(2,1)S(1)} %get-tuple-element.158, bf16[2,14,14,1,3,64]{5,4,2,1,0,3:T(4,128)(2,1)S(1)} %get-tuple-element.159, f32[2,3,14,14,14]{3,4,1,0,2:T(8,128)} %convolution_bitcast_fusion.5), kind=kOutput, calls=%fused_computation.268 | convolution fusion | flops 30424296 | bytes 1359456 | tf_op jit(solution)/shard_map/gabnc,gefnc->gnabef/dot_general | solution.py:50
  86.4 6.1 exponential_reduce_fusion
  92.5 14.1 %copy.290 = f32[2,3,14,14,14,14]{5,4,3,2,1,0:T(8,128)} copy(f32[2,3,14,14,14,14]{3,5,4,2,1,0:T(8,128)} %get-tuple-element.187) | data formatting | bytes 1843968 | tf_op jit(solution)/shard_map/add | solution.py:53
  108.2 7.2 fusion.121
  115.5 6.1 exponential_reduce_fusion.1
  121.7 13.7 %copy.269 = f32[2,3,14,14,14,14]{5,4,3,2,1,0:T(8,128)} copy(f32[2,3,14,14,14,14]{3,5,4,2,1,0:T(8,128)} %get-tuple-element.185) | data formatting | bytes 1843968 | tf_op jit(solution)/shard_map/add | solution.py:53
  135.4 31.2 %all_gather.9 = bf16[192,768]{0,1:T(8,128)(2,1)S(1)} all-gather(bf16[192,96]{0,1:T(8,128)(2,1)S(1)} %copy.276), channel_id=1, replica_groups=mesh['dp'=8,'tensor'=4] {'dp'}, dimensions={1}, use_global_device_ids=true | all-gather | bytes 331776 | tf_op jit(solution)/shard_map/all_gather | solution.py:118
  167.8 6.7 reshape.288
  176.0 6.6 reshape.285
  188.1 54.7 %all-reduce.17.cloned.1.call-done = (f32[392,768]{1,0:T(8,128)}, f32[392,768]{1,0:T(8,128)}) async-done(((f32[392,768]{1,0:T(8,128)}, f32[392,768]{1,0:T(8,128)}), (f32[392,768]{1,0:T(8,128)}, f32[392,768]{1,0:T(8,128)})) %all-reduce.17.cloned.1.call-update) | async-done | bytes 2408464 | tf_op jit(solution)/shard_map/psum | solution.py:62
  248.7 6.3 multiply_convert_fusion.2
  259.8 12.5 %all-gather.5.cloned.1.call-done = bf16[768,768]{0,1:T(8,128)(2,1)} async-done(((bf16[768,96]{0,1:T(8,128)(2,1)}), bf16[768,768]{0,1:T(8,128)(2,1)}) %all-gather.5.cloned.1.call-update) | async-done | bytes 1179664 | tf_op jit(solution)/shard_map/all_gather | solution.py:120
  278.7 19.5 %psum.201 = f32[]{:T(128)} all-reduce(f32[]{:T(128)} %convert_reduce_fusion.6), channel_id=1, replica_groups=mesh['dp'=8,'tensor'=4] {'dp'}, use_global_device_ids=true, to_apply=%region_20.0 | all-reduce | flops 1 | bytes 8 | tf_op jit(solution)/shard_map/psum | solution.py:173
  308.4 24.5 %all-reduce.15.cloned.1.call-done = (f32[392,768]{1,0:T(8,128)}, f32[392,768]{1,0:T(8,128)}) async-done(((f32[392,768]{1,0:T(8,128)}, f32[392,768]{1,0:T(8,128)}), (f32[392,768]{1,0:T(8,128)}, f32[392,768]{1,0:T(8,128)})) %all-reduce.15.cloned.1.call-update) | async-done | bytes 2408464 | tf_op jit(solution)/shard_map/psum | solution.py:62
  356.4 46.0 %all-reduce.13.cloned.1.call-done = (f32[392,768]{1,0:T(8,128)}, f32[392,768]{1,0:T(8,128)}) async-done(((f32[392,768]{1,0:T(8,128)}, f32[392,768]{1,0:T(8,128)}), (f32[392,768]{1,0:T(8,128)}, f32[392,768]{1,0:T(8,128)})) %all-reduce.13.cloned.1.call-update) | async-done | bytes 2408464 | tf_op jit(solution)/shard_map/psum | solution.py:62
  436.9 6.7 reshape.305
  443.6 7.6 %fusion.108 = (f32[2,3,14,14,14]{4,3,2,1,0:T(8,128)}, f32[2,3,14,14,14]{4,3,2,1,0:T(8,128)}) fusion(f32[2,3,14,14,14,14]{5,4,3,2,1,0:T(8,128)} %reshape.305), kind=kLoop, calls=%fused_computation.256 | loop fusion | flops 428064 | bytes 1053696 | tf_op jit(solution)/shard_map/reduce_sum | solution.py:280
  458.2 7.8 %reshape.307 = f32[2,3,14,14,14,14]{5,4,3,2,1,0:T(8,128)} reshape(f32[2,3,196,196]{3,2,1,0:T(8,128)} %copy.328) | data formatting | bytes 1843968 | tf_op jit(solution)/shard_map/reshape | solution.py:277
  466.1 7.5 %fusion.109 = (f32[2,3,14,14,14]{4,3,2,1,0:T(8,128)}, f32[2,3,14,14,14]{4,3,2,1,0:T(8,128)}) fusion(f32[2,3,14,14,14,14]{5,4,3,2,1,0:T(8,128)} %reshape.307), kind=kLoop, calls=%fused_computation.257 | loop fusion | flops 428064 | bytes 1053696 | tf_op jit(solution)/shard_map/reduce_sum | solution.py:280
  556.7 10.7 %all-reduce.1 = (f32[768]{0:T(1024)S(1)}, f32[768]{0:T(1024)S(1)}, f32[768]{0:T(1024)S(1)}, f32[768]{0:T(1024)S(1)}, f32[768]{0:T(1024)S(1)}, /*index=5*/f32[768...) all-reduce(f32[768]{0:T(1024)S(1)} %add.395, ...), channel_id=1, replica_groups=mesh['dp'=8,'tensor'=4] {'tensor'}, use_global_device_ids=true, to_apply=%region_41.0 | all-reduce | flops 8064 | bytes 64512 | tf_op jit(solution)/shard_map/psum | solution.py:326
  567.5 39.1 %all-reduce = (f32[]{:T(128)}, f32[768]{0:T(1024)}, f32[768]{0:T(1024)}, f32[2,192]{1,0:T(2,128)}, f32[768]{0:T(1024)}, /*index=5*/f32[768]{0:T(1024)}, f32[768]...) all-reduce(f32[]{:T(128)S(6)} %add.383, ...), channel_id=1, replica_groups=mesh['dp'=8,'tensor'=4] {'dp'}, use_global_device_ids=true, to_apply=%region_18.0 | all-reduce | flops 9217 | bytes 73736 | tf_op jit(solution)/shard_map/psum | solution.py:173
  619.7 31.2 %reduce-scatter.9.cloned.1.call-done = f32[96,768]{1,0:T(8,128)} async-done(((f32[768,768]{1,0:T(8,128)}), f32[96,768]{1,0:T(8,128)}) %reduce-scatter.9.cloned.1.call-update) | async-done | bytes 294928 | tf_op jit(solution)/shard_map/reduce_scatter | solution.py:323
  650.9 72.3 %reduce-scatter.11.cloned.1.call-done = f32[768,96]{0,1:T(8,128)} async-done(((f32[768,768]{0,1:T(8,128)}), f32[768,96]{0,1:T(8,128)}) %reduce-scatter.11.cloned.1.call-update) | async-done | bytes 294928 | tf_op jit(solution)/shard_map/reduce_scatter | solution.py:324
  (469 shorter events, 225.4 us)
Async XLA Ops:
  8.0 234.8 %all-reduce.17.cloned.1.call-start = ((), (), s32[]{:S(2)}) async-start(), calls=%async_computation.13 | async-start | bytes 4816896 | tf_op jit(solution)/shard_map/psum | solution.py:62
  16.3 57.9 %copy-start.72 = (bf16[14,14,64,1,1]{2,1,4,3,0:T(8,128)(2,1)}, bf16[14,14,64,1,1]{2,1,4,3,0:T(8,128)(2,1)S(1)}, u32[]{:S(2)}) copy-start(bf16[14,14,64,1,1]{2,1,4,3,0:T(8,128)(2,1)S(1)} %fusion.32) | copy-start | bytes 75268
  16.5 56.0 %copy-start.74 = (bf16[14,14,64,1,1]{2,1,4,3,0:T(8,128)(2,1)}, bf16[14,14,64,1,1]{2,1,4,3,0:T(8,128)(2,1)S(1)}, u32[]{:S(2)}) copy-start(bf16[14,14,64,1,1]{2,1,4,3,0:T(8,128)(2,1)S(1)} %fusion.33) | copy-start | bytes 75268
  16.7 46.8 %copy-start.92 = (f32[392]{0:T(512)}, f32[392]{0:T(512)S(1)}, u32[]{:S(2)}) copy-start(f32[392]{0:T(512)S(1)} %div.87) | copy-start | bytes 4708
  16.8 46.5 %copy-start.94 = (f32[392]{0:T(512)}, f32[392]{0:T(512)S(1)}, u32[]{:S(2)}) copy-start(f32[392]{0:T(512)S(1)} %div.79) | copy-start | bytes 4708
  17.0 46.3 %copy-start.96 = (f32[392]{0:T(512)}, f32[392]{0:T(512)S(1)}, u32[]{:S(2)}) copy-start(f32[392]{0:T(512)S(1)} %rsqrt.39) | copy-start | bytes 4708
  17.2 46.3 %copy-start.98 = (f32[392]{0:T(512)}, f32[392]{0:T(512)S(1)}, u32[]{:S(2)}) copy-start(f32[392]{0:T(512)S(1)} %rsqrt.42) | copy-start | bytes 4708
  121.6 44.9 %copy-start.67 = (bf16[2,14,14,1,3,64]{5,4,2,1,0,3:T(4,128)(2,1)S(1)}, bf16[2,14,14,1,3,64]{5,4,2,1,0,3:T(4,128)(2,1)}, u32[]{:S(2)}) copy-start(bf16[2,14,14,1,3,64]{5,4,2,1,0,3:T(4,128)(2,1)} %get-tuple-element.160) | copy-start | bytes 451588
  186.9 56.0 %copy-start.109 = (f32[768]{0:T(1024)S(1)}, f32[768]{0:T(1024)}, u32[]{:S(2)}) copy-start(f32[768]{0:T(1024)} %param.25) | copy-start | bytes 9220
  186.9 61.8 %all-gather.3.cloned.1.call-start = ((), (), s32[]{:S(2)}) async-start(), calls=%async_computation.4 | async-start | bytes 1327104 | tf_op jit(solution)/shard_map/all_gather | solution.py:119
  187.5 84.9 %all-gather.5.cloned.1.call-start = ((), (), s32[]{:S(2)}) async-start(), calls=%async_computation.5 | async-start | bytes 1327104 | tf_op jit(solution)/shard_map/all_gather | solution.py:120
  188.1 144.9 %all-reduce.15.cloned.1.call-start = ((), (), s32[]{:S(2)}) async-start(), calls=%async_computation.12 | async-start | bytes 4816896 | tf_op jit(solution)/shard_map/psum | solution.py:62
  277.5 125.0 %all-reduce.13.cloned.1.call-start = ((), (), s32[]{:S(2)}) async-start(), calls=%async_computation.11 | async-start | bytes 4816896 | tf_op jit(solution)/shard_map/psum | solution.py:62
  345.5 202.9 %reduce-scatter.15.cloned.1.call-start = ((), (), s32[]{:S(2)}) async-start(), calls=%async_computation.9 | async-start | bytes 884736
  424.6 129.7 %all-reduce.11.cloned.1.call-start = ((), (), s32[]{:S(2)}) async-start(), calls=%async_computation.10 | async-start | bytes 4816896 | tf_op jit(solution)/shard_map/psum | solution.py:62
  497.4 120.4 %reduce-scatter.13.cloned.1.call-start = ((), (), s32[]{:S(2)}) async-start(), calls=%async_computation.8 | async-start | bytes 2211840
  511.4 139.5 %reduce-scatter.9.cloned.1.call-start = ((), (), s32[]{:S(2)}) async-start(), calls=%async_computation.6 | async-start | bytes 2654208 | tf_op jit(solution)/shard_map/reduce_scatter | solution.py:323
  517.0 206.2 %reduce-scatter.11.cloned.1.call-start = ((), (), s32[]{:S(2)}) async-start(), calls=%async_computation.7 | async-start | bytes 2654208 | tf_op jit(solution)/shard_map/reduce_scatter | solution.py:324
  547.3 59.3 %copy-start.3 = (f32[392,768]{1,0:T(8,128)S(1)}, f32[392,768]{1,0:T(8,128)}, u32[]{:S(2)}) copy-start(f32[392,768]{1,0:T(8,128)} %copy-done.2) | copy-start | bytes 3612676
  548.1 58.5 %copy-start.1 = (f32[392,768]{1,0:T(8,128)S(1)}, f32[392,768]{1,0:T(8,128)}, u32[]{:S(2)}) copy-start(f32[392,768]{1,0:T(8,128)} %copy-done) | copy-start | bytes 3612676
  548.1 58.5 %copy-start.93 = (f32[392]{0:T(512)S(1)}, f32[392]{0:T(512)}, u32[]{:S(2)}) copy-start(f32[392]{0:T(512)} %copy-done.92) | copy-start | bytes 4708
  548.1 58.5 %copy-start.95 = (f32[392]{0:T(512)S(1)}, f32[392]{0:T(512)}, u32[]{:S(2)}) copy-start(f32[392]{0:T(512)} %copy-done.94) | copy-start | bytes 4708
  548.1 58.5 %copy-start.97 = (f32[392]{0:T(512)S(1)}, f32[392]{0:T(512)}, u32[]{:S(2)}) copy-start(f32[392]{0:T(512)} %copy-done.96) | copy-start | bytes 4708
  548.1 58.5 %copy-start.99 = (f32[392]{0:T(512)S(1)}, f32[392]{0:T(512)}, u32[]{:S(2)}) copy-start(f32[392]{0:T(512)} %copy-done.98) | copy-start | bytes 4708
  (107 other events, 431.6 us)
Sparse Core Ops, SparseCore 0:
  187.0 55.7 all-reduce.16
  277.6 55.3 all-reduce.14
  345.6 56.7 all-reduce.12
  497.5 56.7 all-reduce.10
Sparse Core Ops, SparseCore 1:
  189.8 40.4 all-gather.2
  232.5 39.8 all-gather.4
  424.7 62.5 reduce-scatter.14
  511.5 66.8 reduce-scatter.12
  582.4 68.4 reduce-scatter.8
  655.0 68.2 reduce-scatter.10
where the time goes:
time: 738 us; the launch traced here: 732 us
  waiting for transfers between devices  247 us (33%)
  local copies, waits for them, and re-layouts  154 us (21%)
  blocking collectives  140 us (19%)
  matrix products  88.9 us (12%)
  other arithmetic  79.9 us (11%)
  between operations  21.5 us (3%)
    psum x4, waiting for transfers between devices, row_total(): return lax.psum(partial_value, 'tensor')  130 us
    reduce_scatter x1, waiting for transfers between devices, shards(): lax.psum_scatter(shrink_acc, 'dp', scatter_dimension=1, tiled=True)  72.3 us
    psum x2, blocking collectives, shards(): loss_total, count = lax.psum((local_loss, jnp.sum(live)), 'dp')  58.7 us
    all_gather x1, blocking collectives, shards(): lax.all_gather(triple_weight, 'dp', axis=1, tiled=True)  39.1 us
    unnamed x260, local copies, waits for them, and re-layouts  34.3 us
    reduce_scatter x1, waiting for transfers between devices, shards(): lax.psum_scatter(expand_acc, 'dp', scatter_dimension=0, tiled=True)  31.2 us
    all_gather x1, blocking collectives, shards(): lax.all_gather(output_weight, 'dp', axis=1, tiled=True)  31.2 us
    add x2, local copies, waits for them, and re-layouts, score_block(): scores = scores + along_rows[..., :, None] + along_cols[..., None, :]  27.8 us
  transfers between devices with their start and end apart: 10, of which 7 were waited for; matrix products, arithmetic and copies ran while one was open for 23% of the time, Pallas kernels for 0%

commit v1 on v0

--- a/solution.py
+++ b/solution.py
@@ -3,7 +3,11 @@
 import jax
 import jax.numpy as jnp
 from jax import lax
+from jax.experimental import pallas as pl
+from jax.experimental.pallas import tpu as pltpu
 from jax.sharding import PartitionSpec as P
+
+MESH = pl.DeviceIdType.MESH
 
 D = 768
 HEADS = 12
@@ -65,6 +69,107 @@
 def share_of(values):
     share_rows = values.shape[0] // lax.axis_size("tensor")
     return lax.dynamic_slice_in_dim(values, lax.axis_index("tensor") * share_rows, share_rows, 0)
+
+
+def z_mate(z, k):
+    if k == 1:
+        return z + 1 - 2 * (z % 2)
+    if k == 2:
+        return (z + 2) % 4
+    return 3 - z
+
+
+def gather_kernel(a_in, e_in, s_in, a_out, e_out, s_out, send_sem, recv_sem, local_sem):
+    dp = lax.axis_index("dp")
+    t = lax.axis_index("tensor")
+    z = dp // 2
+    x = dp % 2
+    mates = [(z_mate(z, k) * 2 + x, t) for k in (1, 2, 3)]
+    x_mate = (z * 2 + 1 - x, t)
+    barrier = pltpu.get_barrier_semaphore()
+    for mate in mates + [x_mate]:
+        pl.semaphore_signal(barrier, inc=1, device_id=mate, device_id_type=MESH)
+    pl.semaphore_wait(barrier, 4)
+    ins = (a_in, e_in, s_in)
+    outs = (a_out, e_out, s_out)
+    started = []
+    local = []
+    for g in range(3):
+        for k in (1, 2, 3):
+            copy = pltpu.make_async_remote_copy(
+                src_ref=ins[g],
+                dst_ref=outs[g].at[dp],
+                send_sem=send_sem.at[g, k - 1],
+                recv_sem=recv_sem.at[g, k - 1],
+                device_id=mates[k - 1],
+                device_id_type=MESH,
+            )
+            copy.start()
+            started.append(copy)
+        copy = pltpu.make_async_remote_copy(
+            src_ref=ins[g],
+            dst_ref=outs[g].at[dp],
+            send_sem=send_sem.at[g, 3],
+            recv_sem=recv_sem.at[g, 3],
+            device_id=x_mate,
+            device_id_type=MESH,
+        )
+        copy.start()
+        started.append(copy)
+        own = pltpu.make_async_copy(ins[g], outs[g].at[dp], local_sem.at[g])
+        own.start()
+        local.append(own)
+    for g in range(3):
+        for k in (1, 2, 3):
+            row = z_mate(z, k) * 2 + x
+            started[4 * g + k - 1].wait_recv()
+            copy = pltpu.make_async_remote_copy(
+                src_ref=outs[g].at[row],
+                dst_ref=outs[g].at[row],
+                send_sem=send_sem.at[g, 3 + k],
+                recv_sem=recv_sem.at[g, 3 + k],
+                device_id=x_mate,
+                device_id_type=MESH,
+            )
+            copy.start()
+            started.append(copy)
+    for g in range(3):
+        started[4 * g + 3].wait_recv()
+        local[g].wait()
+    for copy in started[12:]:
+        copy.wait_recv()
+    for copy in started:
+        copy.wait_send()
+
+
+def gather_weights(triple_weight, output_weight, expand_weight, shrink_weight):
+    rows = triple_weight.shape[1]
+    width = triple_weight.shape[2]
+    attention = jnp.concatenate(
+        [triple_weight[0], triple_weight[1], triple_weight[2], output_weight.T], axis=1
+    )
+    shapes = [
+        jax.ShapeDtypeStruct((8,) + part.shape, jnp.bfloat16)
+        for part in (attention, expand_weight, shrink_weight.T)
+    ]
+    spec = pl.BlockSpec(memory_space=pltpu.VMEM)
+    full = pl.pallas_call(
+        gather_kernel,
+        out_shape=shapes,
+        in_specs=[spec] * 3,
+        out_specs=[spec] * 3,
+        scratch_shapes=[
+            pltpu.SemaphoreType.DMA((3, 7)),
+            pltpu.SemaphoreType.DMA((3, 7)),
+            pltpu.SemaphoreType.DMA((3,)),
+        ],
+        compiler_params=pltpu.CompilerParams(
+            collective_id=0, has_side_effects=True, vmem_limit_bytes=32 << 20
+        ),
+    )(attention, expand_weight, shrink_weight.T)
+    attention, expand, shrink_t = (part.reshape(8 * rows, -1) for part in full)
+    triple = jnp.stack([attention[:, i * width : (i + 1) * width] for i in range(3)])
+    return triple, attention[:, 3 * width :].T, expand, shrink_t.T
 
 
 def shards(
@@ -109,16 +214,19 @@
     triple_bias = jnp.stack(
         [query_value_bias[0], jnp.zeros_like(query_value_bias[0]), query_value_bias[1]]
     )
-    saved = []
-    outputs = []
-    local_loss = jnp.zeros((), jnp.float32)
-    for micro in range(MICRO):
+    if lax.axis_size("dp") == 8 and lax.axis_size("tensor") == 4:
+        gathered = gather_weights(triple_weight, output_weight, expand_weight, shrink_weight)
+    else:
         gathered = (
             lax.all_gather(triple_weight, "dp", axis=1, tiled=True),
             lax.all_gather(output_weight, "dp", axis=1, tiled=True),
             lax.all_gather(expand_weight, "dp", axis=0, tiled=True),
             lax.all_gather(shrink_weight, "dp", axis=1, tiled=True),
         )
+    saved = []
+    outputs = []
+    local_loss = jnp.zeros((), jnp.float32)
+    for micro in range(MICRO):
         full_triple, full_output, full_expand, full_shrink = gathered
         lower = micro * win_micro
         flat_rows = inputs[lower : lower + win_micro].reshape(micro_rows, D).astype(jnp.float32)
@@ -189,12 +297,6 @@
     cols_expanded_acc = jnp.zeros((WIN, WIN, HEAD), jnp.float32)
     input_grads = []
     for micro in range(MICRO):
-        gathered = (
-            lax.all_gather(triple_weight, "dp", axis=1, tiled=True),
-            lax.all_gather(output_weight, "dp", axis=1, tiled=True),
-            lax.all_gather(expand_weight, "dp", axis=0, tiled=True),
-            lax.all_gather(shrink_weight, "dp", axis=1, tiled=True),
-        )
         full_triple, full_output, full_expand, full_shrink = gathered
         (
             unit_one,

time: 738 us -> 799 us (1.083)
  blocking collectives: 140 us -> 71.6 us
  Pallas kernels: 0 us -> 50.2 us
  local copies, waits for them, and re-layouts: 154 us -> 189 us
  waiting for transfers between devices: 247 us -> 279 us
    all_gather x2 -> x0, blocking collectives: 70.3 us -> none  [the longest x1 39.1 us: shards(): lax.all_gather(triple_weight, 'dp', axis=1, tiled=True)]
    pallas_call x0 -> x1, Pallas kernels: none -> 50.2 us  [gather_weights(): pl.pallas_call(gather_kernel, out_shape=shapes, in_specs=[spec] * 3, out_...]
    reduce_scatter x1, waiting for transfers between devices: 31.2 us -> 69.8 us  [shards(): lax.psum_scatter(expand_acc, 'dp', scatter_dimension=0, tiled=True)]
    all_gather x2 -> x0, waiting for transfers between devices: 12.5 us -> none  [the longest x1 12.5 us: shards(): lax.all_gather(shrink_weight, 'dp', axis=1, tiled=True)]
    unnamed x260 -> x250, local copies, waits for them, and re-layouts: 34.3 us -> 36.5 us
  transfers between devices with their start and end apart: 10 -> 8, of which waited for: 7 -> 7; matrix products, arithmetic and copies ran while one was open for 23% -> 20% of each run, Pallas kernels for 0% -> 0%
where the time goes in v1:
time: 799 us; the launch traced here: 788 us
  waiting for transfers between devices  279 us (35%)
  local copies, waits for them, and re-layouts  189 us (24%)
  matrix products  92.2 us (12%)
  other arithmetic  84.5 us (11%)
  blocking collectives  71.6 us (9%)
  Pallas kernels  50.2 us (6%)
  between operations  20.3 us (3%)
    psum x4, waiting for transfers between devices, row_total(): return lax.psum(partial_value, 'tensor')  129 us
    reduce_scatter x1, waiting for transfers between devices, shards(): lax.psum_scatter(shrink_acc, 'dp', scatter_dimension=1, tiled=True)  72.1 us
    reduce_scatter x1, waiting for transfers between devices, shards(): lax.psum_scatter(expand_acc, 'dp', scatter_dimension=0, tiled=True)  69.8 us
    psum x2, blocking collectives, shards(): loss_total, count = lax.psum((local_loss, jnp.sum(live)), 'dp')  60.9 us
    pallas_call x1, Pallas kernels, gather_weights(): pl.pallas_call(gather_kernel, out_shape=shapes, in_specs=[spec] * 3, out_...  50.2 us
    unnamed x250, local copies, waits for them, and re-layouts  36.5 us
    add x2, local copies, waits for them, and re-layouts, score_block(): scores = scores + along_rows[..., :, None] + along_cols[..., None, :]  27.7 us
    reshape x4, local copies, waits for them, and re-layouts, score_block(): return scores.reshape(groups, heads, side * side, side * side)  19.5 us
  transfers between devices with their start and end apart: 8, of which 7 were waited for; matrix products, arithmetic and copies ran while one was open for 20% of the time, Pallas kernels for 0%

profile of v1, /device:TPU:0, one launch (start us, length us, event | category | flops | bytes accessed | tf_op | source)
XLA Modules:
  0.0 788.3 jit_solution(17911107092221528538)
XLA Ops:
  23.5 50.2 %shard_map.296 = (bf16[8,96,768]{2,1,0:T(8,128)(2,1)S(1)}, bf16[8,96,768]{2,1,0:T(8,128)(2,1)S(1)}, bf16[8,96,768]{2,1,0:T(8,128)(2,1)S(1)}) custom-call(bf16[96,768]{1,0:T(8,128)(2,1)S(1)} %pad_maximum_fusion.3.a_in, bf16[96,768]{1,0:T(8,128)(2,1)S(1)} %copy-done, bf16[96,768]{1,0:T(8,128)(2,1)S(1)} %bitcast.268), custom_call_target="tpu_custom_call" | custom-call | tf_op jit(solution)/shard_map/pallas_call | solution.py:156
  113.2 8.3 %fusion.129 = (f32[2,3,14,14]{3,2,1,0:T(8,128)}, f32[2,3,14,14,14,14]{3,5,4,2,1,0:T(8,128)}) fusion(f32[2,3,14,14,14]{3,4,2,1,0:T(8,128)} %copy.289, bf16[2,14,14,1,3,64]{5,4,2,1,0,3:T(4,128)(2,1)} %get-tuple-element.164, bf16[2,14,14,1,3,64]{5,4,2,1,0,3:T(4,128)(2,1)} %get-tuple-element.165, f32[2,3,14,14,14]{3,4,1,0,2:T(8,128)} %convolution_bitcast_fusion.5), kind=kOutput, calls=%fused_computation.280 | convolution fusion | flops 30424296 | bytes 1359456 | tf_op jit(solution)/shard_map/gabnc,gefnc->gnabef/dot_general | solution.py:54
  122.4 6.7 exponential_reduce_fusion
  129.1 14.1 %copy.290 = f32[2,3,14,14,14,14]{5,4,3,2,1,0:T(8,128)} copy(f32[2,3,14,14,14,14]{3,5,4,2,1,0:T(8,128)} %get-tuple-element.199) | data formatting | bytes 1843968 | tf_op jit(solution)/shard_map/add | solution.py:57
  145.9 8.3 %fusion.128 = (f32[2,3,14,14]{3,2,1,0:T(8,128)}, f32[2,3,14,14,14,14]{3,5,4,2,1,0:T(8,128)}) fusion(f32[2,3,14,14,14]{3,4,2,1,0:T(8,128)} %copy.270, bf16[2,14,14,1,3,64]{5,4,2,1,0,3:T(4,128)(2,1)} %get-tuple-element.167, bf16[2,14,14,1,3,64]{5,4,2,1,0,3:T(4,128)(2,1)} %copy-done.18, f32[2,3,14,14,14]{3,4,1,0,2:T(8,128)} %convolution_bitcast_fusion.7), kind=kOutput, calls=%fused_computation.279 | convolution fusion | flops 30424296 | bytes 1359456 | tf_op jit(solution)/shard_map/gabnc,gefnc->gnabef/dot_general | solution.py:54
  155.7 6.7 exponential_reduce_fusion.1
  162.4 13.6 %copy.271 = f32[2,3,14,14,14,14]{5,4,3,2,1,0:T(8,128)} copy(f32[2,3,14,14,14,14]{3,5,4,2,1,0:T(8,128)} %get-tuple-element.197) | data formatting | bytes 1843968 | tf_op jit(solution)/shard_map/add | solution.py:57
  185.2 7.5 reshape.300
  201.1 7.6 reshape.295
  215.8 57.0 %all-reduce.17.cloned.1.call-done = (f32[392,768]{1,0:T(8,128)}, f32[392,768]{1,0:T(8,128)}) async-done(((f32[392,768]{1,0:T(8,128)}, f32[392,768]{1,0:T(8,128)}), (f32[392,768]{1,0:T(8,128)}, f32[392,768]{1,0:T(8,128)})) %all-reduce.17.cloned.1.call-update) | async-done | bytes 2408464 | tf_op jit(solution)/shard_map/psum | solution.py:66
  291.6 22.0 %psum.201 = f32[]{:T(128)} all-reduce(f32[]{:T(128)} %convert_reduce_fusion.6), channel_id=1, replica_groups=mesh['dp'=8,'tensor'=4] {'dp'}, use_global_device_ids=true, to_apply=%region_20.0 | all-reduce | flops 1 | bytes 8 | tf_op jit(solution)/shard_map/psum | solution.py:281
  327.6 19.6 %all-reduce.15.cloned.1.call-done = (f32[392,768]{1,0:T(8,128)}, f32[392,768]{1,0:T(8,128)}) async-done(((f32[392,768]{1,0:T(8,128)}, f32[392,768]{1,0:T(8,128)}), (f32[392,768]{1,0:T(8,128)}, f32[392,768]{1,0:T(8,128)})) %all-reduce.15.cloned.1.call-update) | async-done | bytes 2408464 | tf_op jit(solution)/shard_map/psum | solution.py:66
  347.3 5.2 multiply_multiply_fusion.2
  370.0 47.4 %all-reduce.13.cloned.1.call-done = (f32[392,768]{1,0:T(8,128)}, f32[392,768]{1,0:T(8,128)}) async-done(((f32[392,768]{1,0:T(8,128)}, f32[392,768]{1,0:T(8,128)}), (f32[392,768]{1,0:T(8,128)}, f32[392,768]{1,0:T(8,128)})) %all-reduce.13.cloned.1.call-update) | async-done | bytes 2408464 | tf_op jit(solution)/shard_map/psum | solution.py:66
  445.9 7.7 reshape.317
  453.6 7.6 fusion.114
  468.9 7.9 reshape.319
  476.7 7.5 fusion.115
  559.9 5.0 all-reduce.11.cloned.1.call-done
  567.3 10.7 %all-reduce.1 = (f32[768]{0:T(1024)S(1)}, f32[768]{0:T(1024)S(1)}, f32[768]{0:T(1024)S(1)}, f32[768]{0:T(1024)S(1)}, f32[768]{0:T(1024)S(1)}, /*index=5*/f32[768...) all-reduce(f32[768]{0:T(1024)S(1)} %add.395, ...), channel_id=1, replica_groups=mesh['dp'=8,'tensor'=4] {'tensor'}, use_global_device_ids=true, to_apply=%region_41.0 | all-reduce | flops 8064 | bytes 64512 | tf_op jit(solution)/shard_map/psum | solution.py:428
  578.1 38.9 %all-reduce = (f32[]{:T(128)}, f32[768]{0:T(1024)}, f32[768]{0:T(1024)}, f32[2,192]{1,0:T(2,128)}, f32[768]{0:T(1024)}, /*index=5*/f32[768]{0:T(1024)}, f32[768]...) all-reduce(f32[]{:T(128)S(6)} %add.383, ...), channel_id=1, replica_groups=mesh['dp'=8,'tensor'=4] {'dp'}, use_global_device_ids=true, to_apply=%region_18.0 | all-reduce | flops 9217 | bytes 73736 | tf_op jit(solution)/shard_map/psum | solution.py:281
  628.1 8.2 %reduce-scatter.13.cloned.1.call-done = f32[96,576]{1,0:T(8,128)} async-done(((f32[768,576]{1,0:T(8,128)}), f32[96,576]{1,0:T(8,128)}) %reduce-scatter.13.cloned.1.call-update) | async-done | bytes 221200
  638.1 69.8 %reduce-scatter.9.cloned.1.call-done = f32[96,768]{1,0:T(8,128)} async-done(((f32[768,768]{1,0:T(8,128)}), f32[96,768]{1,0:T(8,128)}) %reduce-scatter.9.cloned.1.call-update) | async-done | bytes 294928 | tf_op jit(solution)/shard_map/reduce_scatter | solution.py:425
  707.9 72.1 %reduce-scatter.11.cloned.1.call-done = f32[768,96]{0,1:T(8,128)} async-done(((f32[768,768]{0,1:T(8,128)}), f32[768,96]{0,1:T(8,128)}) %reduce-scatter.11.cloned.1.call-update) | async-done | bytes 294928 | tf_op jit(solution)/shard_map/reduce_scatter | solution.py:426
  (455 shorter events, 258.3 us)
Async XLA Ops:
  7.2 265.6 %all-reduce.17.cloned.1.call-start = ((), (), s32[]{:S(2)}) async-start(), calls=%async_computation.11 | async-start | bytes 4816896 | tf_op jit(solution)/shard_map/psum | solution.py:66
  17.3 64.8 %copy-start.78 = (f32[392]{0:T(512)}, f32[392]{0:T(512)S(1)}, u32[]{:S(2)}) copy-start(f32[392]{0:T(512)S(1)} %div.87) | copy-start | bytes 4708
  17.4 63.2 %copy-start.80 = (f32[392]{0:T(512)}, f32[392]{0:T(512)S(1)}, u32[]{:S(2)}) copy-start(f32[392]{0:T(512)S(1)} %div.79) | copy-start | bytes 4708
  17.6 63.0 %copy-start.82 = (f32[392]{0:T(512)}, f32[392]{0:T(512)S(1)}, u32[]{:S(2)}) copy-start(f32[392]{0:T(512)S(1)} %rsqrt.39) | copy-start | bytes 4708
  17.8 64.3 %copy-start.84 = (f32[392]{0:T(512)}, f32[392]{0:T(512)S(1)}, u32[]{:S(2)}) copy-start(f32[392]{0:T(512)S(1)} %rsqrt.42) | copy-start | bytes 4708
  122.4 70.3 %copy-start.90 = (f32[2,3,196]{2,1,0:T(4,128)}, f32[2,3,196]{2,1,0:T(4,128)S(1)}, u32[]{:S(2)}) copy-start(f32[2,3,196]{2,1,0:T(4,128)S(1)} %reshape.344) | copy-start | bytes 14116
  201.1 7.7 copy-start.92
  215.8 57.1 %copy-start.102 = (f32[768]{0:T(1024)S(1)}, f32[768]{0:T(1024)}, u32[]{:S(2)}) copy-start(f32[768]{0:T(1024)} %param.25) | copy-start | bytes 9220
  215.8 131.5 %all-reduce.15.cloned.1.call-start = ((), (), s32[]{:S(2)}) async-start(), calls=%async_computation.10 | async-start | bytes 4816896 | tf_op jit(solution)/shard_map/psum | solution.py:66
  290.3 127.1 %all-reduce.13.cloned.1.call-start = ((), (), s32[]{:S(2)}) async-start(), calls=%async_computation.9 | async-start | bytes 4816896 | tf_op jit(solution)/shard_map/psum | solution.py:66
  360.4 197.8 %reduce-scatter.15.cloned.1.call-start = ((), (), s32[]{:S(2)}) async-start(), calls=%async_computation.7 | async-start | bytes 884736
  367.0 50.4 %copy-start.3 = (f32[392,768]{1,0:T(8,128)S(1)}, f32[392,768]{1,0:T(8,128)}, u32[]{:S(2)}) copy-start(f32[392,768]{1,0:T(8,128)} %copy-done.2) | copy-start | bytes 3612676
  367.0 50.4 %copy-start.87 = (f32[392]{0:T(512)S(1)}, f32[392]{0:T(512)}, u32[]{:S(2)}) copy-start(f32[392]{0:T(512)} %copy-done.86) | copy-start | bytes 4708
  367.0 50.4 %copy-start.89 = (f32[392]{0:T(512)S(1)}, f32[392]{0:T(512)}, u32[]{:S(2)}) copy-start(f32[392]{0:T(512)} %copy-done.88) | copy-start | bytes 4708
  436.0 128.9 %all-reduce.11.cloned.1.call-start = ((), (), s32[]{:S(2)}) async-start(), calls=%async_computation.8 | async-start | bytes 4816896 | tf_op jit(solution)/shard_map/psum | solution.py:66
  508.0 128.2 %reduce-scatter.13.cloned.1.call-start = ((), (), s32[]{:S(2)}) async-start(), calls=%async_computation.6 | async-start | bytes 2211840
  521.6 186.4 %reduce-scatter.9.cloned.1.call-start = ((), (), s32[]{:S(2)}) async-start(), calls=%async_computation.4 | async-start | bytes 2654208 | tf_op jit(solution)/shard_map/reduce_scatter | solution.py:425
  527.0 253.1 %reduce-scatter.11.cloned.1.call-start = ((), (), s32[]{:S(2)}) async-start(), calls=%async_computation.5 | async-start | bytes 2654208 | tf_op jit(solution)/shard_map/reduce_scatter | solution.py:426
  557.2 59.8 %copy-start.8 = (f32[392,768]{1,0:T(8,128)S(1)}, f32[392,768]{1,0:T(8,128)}, u32[]{:S(2)}) copy-start(f32[392,768]{1,0:T(8,128)} %reshape.313) | copy-start | bytes 3612676
  557.9 59.1 %copy-start.6 = (f32[392,768]{1,0:T(8,128)S(1)}, f32[392,768]{1,0:T(8,128)}, u32[]{:S(2)}) copy-start(f32[392,768]{1,0:T(8,128)} %reshape.312) | copy-start | bytes 3612676
  557.9 59.1 %copy-start.79 = (f32[392]{0:T(512)S(1)}, f32[392]{0:T(512)}, u32[]{:S(2)}) copy-start(f32[392]{0:T(512)} %copy-done.78) | copy-start | bytes 4708
  557.9 59.1 %copy-start.81 = (f32[392]{0:T(512)S(1)}, f32[392]{0:T(512)}, u32[]{:S(2)}) copy-start(f32[392]{0:T(512)} %copy-done.80) | copy-start | bytes 4708
  557.9 59.1 %copy-start.83 = (f32[392]{0:T(512)S(1)}, f32[392]{0:T(512)}, u32[]{:S(2)}) copy-start(f32[392]{0:T(512)} %copy-done.82) | copy-start | bytes 4708
  557.9 59.1 %copy-start.85 = (f32[392]{0:T(512)S(1)}, f32[392]{0:T(512)}, u32[]{:S(2)}) copy-start(f32[392]{0:T(512)} %copy-done.84) | copy-start | bytes 4708
  (99 other events, 228.8 us)
Sparse Core Ops, SparseCore 0:
  215.9 56.8 all-reduce.16
  290.4 56.7 all-reduce.14
  360.5 56.8 all-reduce.12
  436.1 62.4 reduce-scatter.14
  508.1 56.7 all-reduce.10
  568.7 67.5 reduce-scatter.12
  640.3 67.5 reduce-scatter.8
  712.0 68.0 reduce-scatter.10

commit v2 on v0

--- a/solution.py
+++ b/solution.py
@@ -2,8 +2,13 @@
 
 import jax
 import jax.numpy as jnp
+import numpy as np
 from jax import lax
+from jax.experimental import pallas as pl
+from jax.experimental.pallas import tpu as pltpu
 from jax.sharding import PartitionSpec as P
+
+MESH = pl.DeviceIdType.MESH
 
 D = 768
 HEADS = 12
@@ -372,6 +377,794 @@
     )
 
 
+ROWS = 208
+KEYS = 256
+CHUNKS = ((0, 112), (112, 96))
+F32 = jnp.float32
+BF16 = jnp.bfloat16
+
+
+def z_mate(z, k):
+    if k == 0:
+        return z
+    if k == 1:
+        return z + 1 - 2 * (z % 2)
+    if k == 2:
+        return (z + 2) % 4
+    return 3 - z
+
+
+def dot_nn(a, b):
+    return lax.dot_general(a, b, (((1,), (0,)), ((), ())), preferred_element_type=F32)
+
+
+def dot_nt(a, b):
+    return lax.dot_general(a, b, (((1,), (1,)), ((), ())), preferred_element_type=F32)
+
+
+def dot_tn(a, b):
+    return lax.dot_general(a, b, (((0,), (0,)), ((), ())), preferred_element_type=F32)
+
+
+def column_sum(values):
+    return jnp.sum(values, axis=0, keepdims=True)
+
+
+UNITS = ((0, 1, 2, 0, 0), (0, 1, 2, 1, 1), (3, 5, 6, 0, 1))
+
+
+def block_kernel(
+    x_in,
+    target_in,
+    valid_in,
+    vectors,
+    side_in,
+    wa_in,
+    we_in,
+    ws_in,
+    tables_in,
+    onehot,
+    place,
+    pick,
+    block_out,
+    grad_out,
+    ga_out,
+    ge_out,
+    gs_out,
+    small_out,
+    table_out,
+    wa,
+    we,
+    ws,
+    side,
+    xf,
+    unit1,
+    unit2,
+    inv1,
+    inv2,
+    mid,
+    acc,
+    n1,
+    n2,
+    gr,
+    gm,
+    pj,
+    ps,
+    mx,
+    mxr,
+    hid,
+    hidr,
+    slope,
+    gb,
+    gbr,
+    gmx,
+    gp,
+    gpr,
+    t2,
+    tg,
+    es,
+    er,
+    gw,
+    xs,
+    xr,
+    zs,
+    zr,
+    ig,
+    cnt,
+    cntr,
+    sb,
+    sbr,
+    tb,
+    tbr,
+    send_sem,
+    recv_sem,
+):
+    dp = lax.axis_index("dp")
+    t = lax.axis_index("tensor")
+    z = dp // 2
+    x = dp % 2
+    y = t // 2
+    c = t % 2
+    z_mates = [(z_mate(z, k) * 2 + x, t) for k in (1, 2, 3)]
+    x_mate = (z * 2 + 1 - x, t)
+    y_mate = (dp, (1 - y) * 2 + c)
+    c_mate = (dp, y * 2 + 1 - c)
+    peer_window = (1 - y) * 2 + c
+    token_total = lax.axis_size("dp") * 4 * WIN_TOK
+
+    started = []
+
+    def send(src, dst, mate):
+        i = len(started)
+        copy = pltpu.make_async_remote_copy(
+            src_ref=src,
+            dst_ref=dst,
+            send_sem=send_sem.at[i],
+            recv_sem=recv_sem.at[i],
+            device_id=mate,
+            device_id_type=MESH,
+        )
+        copy.start()
+        started.append(copy)
+        return copy
+
+    barrier = pltpu.get_barrier_semaphore()
+    for mate in z_mates + [x_mate, y_mate, c_mate]:
+        pl.semaphore_signal(barrier, inc=1, device_id=mate, device_id_type=MESH)
+    pl.semaphore_wait(barrier, 6)
+
+    w_in = (wa_in, we_in, ws_in)
+    w_full = (wa, we, ws)
+    from_z = {}
+    from_x = {}
+    from_c = {}
+
+    def row_of(k, xx):
+        return z_mate(z, k) * 2 + xx
+
+    def gather_start(g):
+        for k in (1, 2, 3):
+            from_z[g, k] = send(w_in[g], w_full[g].at[0, dp], z_mates[k - 1])
+        from_x[g, 0] = send(w_in[g], w_full[g].at[0, dp], x_mate)
+        from_c[g, 0] = send(w_in[g], w_full[g].at[1, dp], c_mate)
+        w_full[g][0, dp] = w_in[g][...]
+
+    def gather_z(g, k):
+        from_z[g, k].wait_recv()
+        block = w_full[g].at[0, row_of(k, x)]
+        from_x[g, k] = send(block, block, x_mate)
+        from_c[g, k] = send(block, w_full[g].at[1, row_of(k, x)], c_mate)
+
+    def gather_x(g, k):
+        from_x[g, k].wait_recv()
+        from_c[g, 4 + k] = send(
+            w_full[g].at[0, row_of(k, 1 - x)], w_full[g].at[1, row_of(k, 1 - x)], c_mate
+        )
+
+    def gather_end(g):
+        for k in range(8):
+            from_c[g, k].wait_recv()
+
+    gather_start(0)
+    side_copy = send(side_in, side.at[1], c_mate)
+    side[0] = side_in[...]
+    marks_all = valid_in[...].astype(F32)
+    cnt[0] = jnp.full((8, 128), jnp.sum(marks_all), F32)
+    cnt_x = send(cnt.at[0], cntr.at[0], x_mate)
+
+    gain1 = vectors[0:1, :]
+    shift1 = vectors[1:2, :]
+    bias_out = vectors[2:3, :]
+    gain2 = vectors[3:4, :]
+    shift2 = vectors[4:5, :]
+    bias_shrink = vectors[5:6, :]
+
+    lane = lax.broadcasted_iota(jnp.int32, (1, 128), 1)
+    half = ((lane < 64).astype(F32), (lane >= 64).astype(F32))
+    key_mask = [(m * 0.125).astype(BF16) for m in half]
+    half = [m.astype(BF16) for m in half]
+    key_lane = lax.broadcasted_iota(jnp.int32, (1, KEYS), 1)
+    key_bias = jnp.where(key_lane < WIN_TOK, 0.0, -1e30).astype(F32)
+
+    row_ids = lax.broadcasted_iota(jnp.int32, (4, WIN_TOK), 0)
+    own_marks = column_sum(jnp.where(row_ids == t, marks_all, 0.0))
+    eye = lax.broadcasted_iota(jnp.int32, (ROWS, WIN_TOK), 0) == lax.broadcasted_iota(
+        jnp.int32, (ROWS, WIN_TOK), 1
+    )
+    live = jnp.sum(jnp.where(eye, own_marks, 0.0), axis=1, keepdims=True)
+
+    xf[...] = jnp.zeros_like(xf)
+    xf[0, 0:WIN_TOK, :] = x_in[t].astype(F32)
+    xf[1, 0:WIN_TOK, :] = x_in[peer_window].astype(F32)
+    for w in range(2):
+        unit, inverse = normalize(xf[w])
+        n1[0, w] = (unit * gain1 + shift1).astype(BF16)
+        if w == 0:
+            unit1[...] = unit
+            inv1[...] = inverse
+    n1_copy = send(n1.at[0], n1.at[1], c_mate)
+    for p in range(2):
+        t2[p] = dot_nn(onehot[...], tables_in[p]).astype(BF16)
+    pj[:, :, ROWS:, :] = jnp.zeros((2, 2, KEYS - ROWS, 896), BF16)
+    tg[...] = jnp.zeros_like(tg)
+
+    for k in (1, 2, 3):
+        gather_z(0, k)
+    gather_start(1)
+    for k in range(4):
+        gather_x(0, k)
+    cnt_x.wait_recv()
+    cnt[1] = cnt[0] + cntr[0]
+    cnt_z = [send(cnt.at[1], cntr.at[k], z_mates[k - 1]) for k in (1, 2, 3)]
+    side_copy.wait_recv()
+    gather_end(0)
+
+    def project(w):
+        def body(j, carry):
+            value = dot_nn(n1[0, w], wa[j, :, :, 0:640].reshape(D, 640)) + side[j, 1:2, 0:640]
+            pj[w, j, 0:ROWS, 0:640] = value.astype(BF16)
+            rolled = pltpu.roll(value[:, 384:512], 64, 1)
+            pj[w, j, 0:ROWS, 640:768] = rolled.astype(BF16)
+            rolled = pltpu.roll(value[:, 512:640], 64, 1)
+            pj[w, j, 0:ROWS, 768:896] = rolled.astype(BF16)
+            return carry
+
+        lax.fori_loop(0, 2, body, 0)
+
+    def unit_of(w, j, h):
+        q, k, v, p, pv = UNITS[h]
+        query = pj[w, j, 0:ROWS, 128 * q : 128 * q + 128]
+        key = pj[w, j, :, 128 * k : 128 * k + 128] * key_mask[p]
+        value = pj[w, j, :, 128 * v : 128 * v + 128] * half[pv]
+        return query, key, value
+
+    def attend(w):
+        def body(j, carry):
+            mixes = []
+            for h in range(3):
+                query, key, value = unit_of(w, j, h)
+                along = dot_nt(query, t2[UNITS[h][3]]) * place[...]
+                high = along.astype(BF16)
+                low = (along - high.astype(F32)).astype(BF16)
+                scores = dot_nt(query, key) + dot_nn(high, pick[...]) + dot_nn(low, pick[...])
+                scores = scores + key_bias
+                raised = jnp.exp(scores - jnp.max(scores, axis=-1, keepdims=True))
+                soft = raised * (1.0 / jnp.sum(raised, axis=-1, keepdims=True))
+                ps[w, j, h] = soft
+                mixes.append(dot_nn(soft.astype(BF16), value))
+            mx[j, w, :, 0:128] = mixes[2].astype(BF16)
+            mx[j, w, :, 128:256] = (mixes[0] + mixes[1]).astype(BF16)
+            return carry
+
+        lax.fori_loop(0, 2, body, 0)
+
+    def attended(w, lo, n):
+        return dot_nt(mx[0, w, lo : lo + n, :], wa[0, :, :, 512:768].reshape(D, 256)) + dot_nt(
+            mx[1, w, lo : lo + n, :], wa[1, :, :, 512:768].reshape(D, 256)
+        )
+
+    project(1)
+    attend(1)
+    e1 = []
+    for lo, n in CHUNKS:
+        es[0, lo : lo + n, :] = attended(1, lo, n).astype(BF16)
+        e1.append(send(es.at[0, pl.ds(lo, n)], er.at[0, pl.ds(lo, n)], y_mate))
+    for k in (1, 2, 3):
+        gather_z(1, k)
+    gather_start(2)
+    project(0)
+    for k in range(4):
+        gather_x(1, k)
+    attend(0)
+    mx_copy = send(mx.at[1], mxr, c_mate)
+    mid[...] = xf[0] + bias_out + attended(0, 0, ROWS)
+    gather_end(1)
+    for k in (1, 2, 3):
+        gather_z(2, k)
+
+    e2 = []
+    n2_c = []
+    for i, (lo, n) in enumerate(CHUNKS):
+        e1[i].wait_recv()
+        middle = mid[lo : lo + n, :] + er[0, lo : lo + n, :].astype(F32)
+        mid[lo : lo + n, :] = middle
+        unit, inverse = normalize(middle)
+        unit2[lo : lo + n, :] = unit
+        inv2[lo : lo + n, :] = inverse
+        n2[0, 0, lo : lo + n, :] = (unit * gain2 + shift2).astype(BF16)
+        rows = pl.ds(lo, n)
+        e2.append(send(n2.at[0, 0, rows], n2.at[0, 1, rows], y_mate))
+        n2_c.append(send(n2.at[0, 0, rows], n2.at[1, 0, rows], c_mate))
+
+    def feed(w, lo, n):
+        def body(j, carry):
+            before = dot_nn(n2[0, w, lo : lo + n, :], we[j].reshape(D, D)) + side[j, 0:1, :]
+            phi = 0.5 * (1.0 + lax.erf(before * math.sqrt(0.5)))
+            hid[j, w, lo : lo + n, :] = (before * phi).astype(BF16)
+            bell = jnp.exp(-0.5 * before * before) * (1.0 / math.sqrt(2.0 * math.pi))
+            slope[j, w, lo : lo + n, :] = phi + before * bell
+            return carry
+
+        lax.fori_loop(0, 2, body, 0)
+
+    def shrunk(w, lo, n):
+        return dot_nt(hid[0, w, lo : lo + n, :], ws[0].reshape(D, D)) + dot_nt(
+            hid[1, w, lo : lo + n, :], ws[1].reshape(D, D)
+        )
+
+    for lo, n in CHUNKS:
+        feed(0, lo, n)
+    for k in range(4):
+        gather_x(2, k)
+    gather_end(2)
+    e3 = []
+    for i, (lo, n) in enumerate(CHUNKS):
+        rows = pl.ds(lo, n)
+        e2[i].wait_recv()
+        n2_c.append(send(n2.at[0, 1, rows], n2.at[1, 1, rows], c_mate))
+        feed(1, lo, n)
+        es[1, lo : lo + n, :] = shrunk(1, lo, n).astype(BF16)
+        e3.append(send(es.at[1, rows], er.at[1, rows], y_mate))
+    hid_copy = send(hid.at[1], hidr, c_mate)
+    acc[...] = mid[...] + bias_shrink + shrunk(0, 0, ROWS)
+
+    for copy in cnt_z:
+        copy.wait_recv()
+    count = (cnt[1] + cntr[1]) + (cntr[2] + cntr[3])
+    count = count[0:1, 0:1]
+    scaled_live = live * (token_total / count)
+    xf[1, 0:WIN_TOK, :] = target_in[t].astype(F32)
+    xf[1, WIN_TOK:, :] = jnp.zeros((ROWS - WIN_TOK, D), F32)
+    e4 = []
+    gr_c = []
+    loss_part = jnp.zeros((1, D), F32)
+    shrink_bias_part = jnp.zeros((1, D), F32)
+    for i, (lo, n) in enumerate(CHUNKS):
+        rows = pl.ds(lo, n)
+        e3[i].wait_recv()
+        result = acc[lo : lo + n, :] + er[1, lo : lo + n, :].astype(F32)
+        gap = result - xf[1, lo : lo + n, :]
+        grad = gap * scaled_live[lo : lo + n, :]
+        acc[lo : lo + n, :] = grad
+        gr[0, 0, lo : lo + n, :] = grad.astype(BF16)
+        e4.append(send(gr.at[0, 0, rows], gr.at[0, 1, rows], y_mate))
+        gr_c.append(send(gr.at[0, 0, rows], gr.at[1, 0, rows], c_mate))
+        block_out[t, lo : lo + n, :] = result.astype(BF16)
+        loss_part = loss_part + column_sum(gap * gap * live[lo : lo + n, :])
+        shrink_bias_part = shrink_bias_part + column_sum(grad)
+    sb[0] = jnp.zeros((16, D), F32)
+    sb[0, 6:7, :] = loss_part
+    sb[0, 0:1, :] = shrink_bias_part
+
+    def feed_back(w, lo, n):
+        def body(j, carry):
+            grad = dot_nn(gr[0, w, lo : lo + n, :], ws[j].reshape(D, D))
+            grad = grad * slope[j, w, lo : lo + n, :]
+            gb[j, w, lo : lo + n, :] = grad.astype(BF16)
+            return carry
+
+        lax.fori_loop(0, 2, body, 0)
+
+    def expanded_back(w, lo, n):
+        return dot_nt(gb[0, w, lo : lo + n, :], we[0].reshape(D, D)) + dot_nt(
+            gb[1, w, lo : lo + n, :], we[1].reshape(D, D)
+        )
+
+    def rows_of(ref, width):
+        return ref[...].reshape(2 * ROWS, width)
+
+    def weight_grad(g, left, mine, theirs, width, at):
+        value = dot_tn(rows_of(left.at[0], D), rows_of(mine, width)) + dot_tn(
+            rows_of(left.at[1], D), rows_of(theirs, width)
+        )
+        gw[g, :, :, at : at + width] = value.reshape(8, 96, width)
+
+    to_x = {}
+    to_z = {}
+
+    def scatter_x(g):
+        for k in (1, 2, 3, 0):
+            xs[g, k] = gw[g, row_of(k, 1 - x)].astype(BF16)
+            to_x[g, k] = send(xs.at[g, k], xr.at[g, k], x_mate)
+
+    def scatter_z(g):
+        for k in (1, 2, 3):
+            to_x[g, k].wait_recv()
+            total = gw[g, row_of(k, x)] + xr[g, k].astype(F32)
+            zs[g, k - 1] = total.astype(BF16)
+            to_z[g, k] = send(zs.at[g, k - 1], zr.at[g, k - 1], z_mates[k - 1])
+
+    def scatter_end(g, out):
+        to_x[g, 0].wait_recv()
+        total = gw[g, dp] + xr[g, 0].astype(F32)
+        for k in (1, 2, 3):
+            to_z[g, k].wait_recv()
+            total = total + zr[g, k - 1].astype(F32)
+        out[...] = total
+
+    for lo, n in CHUNKS:
+        feed_back(0, lo, n)
+    e5 = []
+    for i, (lo, n) in enumerate(CHUNKS):
+        rows = pl.ds(lo, n)
+        e4[i].wait_recv()
+        gr_c.append(send(gr.at[0, 1, rows], gr.at[1, 1, rows], c_mate))
+        feed_back(1, lo, n)
+        es[2, lo : lo + n, :] = expanded_back(1, lo, n).astype(BF16)
+        e5.append(send(es.at[2, rows], er.at[2, rows], y_mate))
+    gb_copy = send(gb.at[1], gbr, c_mate)
+    mid[...] = expanded_back(0, 0, ROWS)
+    for copy in gr_c:
+        copy.wait_recv()
+    hid_copy.wait_recv()
+    weight_grad(2, gr, hid.at[0], hidr, D, 0)
+    scatter_x(2)
+
+    e6 = []
+    gm_c = []
+    gain_part = jnp.zeros((1, D), F32)
+    shift_part = jnp.zeros((1, D), F32)
+    bias_part = jnp.zeros((1, D), F32)
+    for i, (lo, n) in enumerate(CHUNKS):
+        rows = pl.ds(lo, n)
+        e5[i].wait_recv()
+        grad = mid[lo : lo + n, :] + er[2, lo : lo + n, :].astype(F32)
+        unit = unit2[lo : lo + n, :]
+        gain_part = gain_part + column_sum(grad * unit)
+        shift_part = shift_part + column_sum(grad)
+        grad = acc[lo : lo + n, :] + normalize_back(grad, unit, inv2[lo : lo + n, :], gain2)
+        acc[lo : lo + n, :] = grad
+        gm[0, 0, lo : lo + n, :] = grad.astype(BF16)
+        e6.append(send(gm.at[0, 0, rows], gm.at[0, 1, rows], y_mate))
+        gm_c.append(send(gm.at[0, 0, rows], gm.at[1, 0, rows], c_mate))
+        bias_part = bias_part + column_sum(grad)
+    sb[0, 1:2, :] = gain_part
+    sb[0, 2:3, :] = shift_part
+    sb[0, 3:4, :] = bias_part
+
+    bo_y = send(block_out.at[t], block_out.at[t], y_mate)
+    bo_c = [send(block_out.at[t], block_out.at[t], c_mate)]
+    gb_copy.wait_recv()
+    for copy in n2_c:
+        copy.wait_recv()
+    weight_grad(1, n2, gb.at[0], gbr, D, 0)
+    ones = jnp.ones((8, 2 * ROWS), BF16)
+    sb[0, 8:9, :] = (dot_nn(ones, rows_of(gb.at[0], D)) + dot_nn(ones, rows_of(gbr, D)))[0:1]
+    scatter_x(1)
+    scatter_z(2)
+
+    def mixed_back(w, lo, n):
+        for j in range(2):
+            grad = dot_nn(gm[0, w, lo : lo + n, :], wa[j, :, :, 512:768].reshape(D, 256))
+            gmx[j, w, lo : lo + n, :] = grad.astype(BF16)
+
+    def attend_back(w):
+        def body(j, carry):
+            grads_q = []
+            grads_k = []
+            grads_v = []
+            for h in range(3):
+                query, key, value = unit_of(w, j, h)
+                p, pv = UNITS[h][3:]
+                grad = gmx[j, w, :, 0:128] if h == 2 else gmx[j, w, :, 128:256]
+                soft = ps[w, j, h]
+                grad_soft = dot_nt(grad, value)
+                delta = jnp.sum(soft * grad_soft, axis=-1, keepdims=True)
+                grad_scores = (soft * (grad_soft - delta)).astype(BF16)
+                grads_v.append(dot_tn(soft.astype(BF16), grad * half[pv])[0:ROWS])
+                grads_k.append(dot_tn(grad_scores, query * key_mask[p])[0:ROWS])
+                part = (dot_nt(grad_scores, pick[...]) * place[...]).astype(BF16)
+                grads_q.append(dot_nn(grad_scores, key) + dot_nn(part, t2[p]))
+                tg[...] += dot_tn(query * half[p], part)
+            gp[j, w, :, 0:128] = (grads_q[0] + grads_q[1]).astype(BF16)
+            gp[j, w, :, 128:256] = (grads_k[0] + grads_k[1]).astype(BF16)
+            gp[j, w, :, 256:384] = (grads_v[0] + grads_v[1]).astype(BF16)
+            gp[j, w, :, 384:512] = (grads_q[2] + pltpu.roll(grads_k[2], 64, 1)).astype(BF16)
+            gp[j, w, :, 512:640] = pltpu.roll(grads_v[2], 64, 1).astype(BF16)
+            return carry
+
+        lax.fori_loop(0, 2, body, 0)
+
+    def projected_back(w, lo, n):
+        return dot_nt(gp[0, w, lo : lo + n, :], wa[0, :, :, 0:640].reshape(D, 640)) + dot_nt(
+            gp[1, w, lo : lo + n, :], wa[1, :, :, 0:640].reshape(D, 640)
+        )
+
+    for i, (lo, n) in enumerate(CHUNKS):
+        rows = pl.ds(lo, n)
+        e6[i].wait_recv()
+        gm_c.append(send(gm.at[0, 1, rows], gm.at[1, 1, rows], c_mate))
+        mixed_back(1, lo, n)
+    attend_back(1)
+    e7 = []
+    for lo, n in CHUNKS:
+        rows = pl.ds(lo, n)
+        es[3, lo : lo + n, :] = projected_back(1, lo, n).astype(BF16)
+        e7.append(send(es.at[3, rows], er.at[3, rows], y_mate))
+    scatter_z(1)
+    mixed_back(0, 0, ROWS)
+    attend_back(0)
+    gp_copy = send(gp.at[1], gpr, c_mate)
+    mid[...] = projected_back(0, 0, ROWS)
+    for copy in gm_c:
+        copy.wait_recv()
+    mx_copy.wait_recv()
+    n1_copy.wait_recv()
+    gp_copy.wait_recv()
+    weight_grad(0, n1, gp.at[0], gpr, 640, 0)
+    value = dot_tn(rows_of(gm.at[0], D), rows_of(mx.at[0], 256)) + dot_tn(
+        rows_of(gm.at[1], D), rows_of(mxr, 256)
+    )
+    value = value.reshape(8, 96, 256)
+    gw[0, :, :, 512:640] += value[:, :, 0:128]
+    gw[0, :, :, 640:768] = value[:, :, 128:256]
+    scatter_x(0)
+    sb[0, 9:10, 0:640] = (dot_nn(ones, rows_of(gp.at[0], 640)) + dot_nn(ones, rows_of(gpr, 640)))[
+        0:1
+    ]
+
+    e8 = []
+    ig_c = []
+    gain_part = jnp.zeros((1, D), F32)
+    shift_part = jnp.zeros((1, D), F32)
+    for i, (lo, n) in enumerate(CHUNKS):
+        rows = pl.ds(lo, n)
+        e7[i].wait_recv()
+        grad = mid[lo : lo + n, :] + er[3, lo : lo + n, :].astype(F32)
+        unit = unit1[lo : lo + n, :]
+        gain_part = gain_part + column_sum(grad * unit)
+        shift_part = shift_part + column_sum(grad)
+        grad = acc[lo : lo + n, :] + normalize_back(grad, unit, inv1[lo : lo + n, :], gain1)
+        grad_out[t, lo : lo + n, :] = grad.astype(BF16)
+        e8.append(send(grad_out.at[t, rows], grad_out.at[t, rows], y_mate))
+        ig_c.append(send(grad_out.at[t, rows], grad_out.at[t, rows], c_mate))
+    sb[0, 4:5, :] = gain_part
+    sb[0, 5:6, :] = shift_part
+
+    spread = tg[...]
+    spread_high = spread.astype(BF16)
+    spread_low = (spread - spread_high.astype(F32)).astype(BF16)
+    table = dot_nn(spread_high, onehot[...]) + dot_nn(spread_low, onehot[...])
+    tb[0] = table[0:64] + table[64:128]
+    s_c = send(sb.at[0, pl.ds(0, 8)], sbr.at[0, pl.ds(0, 8)], c_mate)
+    t_c = send(tb.at[0], tbr.at[0], c_mate)
+    s_c.wait_recv()
+    t_c.wait_recv()
+    sb[1] = sb[0]
+    sb[1, 0:8, :] = sb[0, 0:8, :] + sbr[0, 0:8, :]
+    tb[1] = tb[0] + tbr[0]
+    s_y = send(sb.at[1, pl.ds(0, 8)], sbr.at[1, pl.ds(0, 8)], y_mate)
+    t_y = send(tb.at[1], tbr.at[1], y_mate)
+    s_y.wait_recv()
+    t_y.wait_recv()
+    sb[2] = sb[1]
+    sb[2, 0:8, :] = sb[1, 0:8, :] + sbr[1, 0:8, :]
+    tb[2] = tb[1] + tbr[1]
+    s_x = send(sb.at[2], sbr.at[2], x_mate)
+    t_x = send(tb.at[2], tbr.at[2], x_mate)
+    scatter_z(0)
+    s_x.wait_recv()
+    t_x.wait_recv()
+    sb[3] = sb[2] + sbr[2]
+    tb[3] = tb[2] + tbr[2]
+    s_z = [send(sb.at[3], sbr.at[2 + k], z_mates[k - 1]) for k in (1, 2, 3)]
+    t_z = [send(tb.at[3], tbr.at[2 + k], z_mates[k - 1]) for k in (1, 2, 3)]
+
+    bo_y.wait_recv()
+    bo_c.append(send(block_out.at[peer_window], block_out.at[peer_window], c_mate))
+    for i, (lo, n) in enumerate(CHUNKS):
+        rows = pl.ds(lo, n)
+        e8[i].wait_recv()
+        ig_c.append(send(grad_out.at[peer_window, rows], grad_out.at[peer_window, rows], c_mate))
+    scatter_end(2, gs_out)
+    scatter_end(1, ge_out)
+    scatter_end(0, ga_out)
+    for copy in s_z + t_z:
+        copy.wait_recv()
+    total = (sb[3] + sbr[3]) + (sbr[4] + sbr[5])
+    small_out[...] = total
+    small_out[6:7, :] = jnp.broadcast_to(
+        jnp.sum(total[6:7, :], axis=1, keepdims=True) / (count * float(D)), (1, D)
+    )
+    table_out[...] = ((tb[3] + tbr[3]) + (tbr[4] + tbr[5])).T
+    for copy in bo_c + ig_c:
+        copy.wait_recv()
+    for copy in started:
+        copy.wait_send()
+
+
+def constant_tables():
+    onehot = np.zeros((512, 64), np.float32)
+    place = np.zeros((ROWS, 512), np.float32)
+    pick = np.zeros((512, KEYS), np.float32)
+    for first in range(WIN):
+        for second in range(WIN):
+            at = first * WIN + second
+            onehot[at, first - second + WIN - 1] = 1.0
+            onehot[256 + at, 27 + first - second + WIN - 1] = 1.0
+            for other in range(WIN):
+                place[first * WIN + other, at] = 1.0
+                place[other * WIN + first, 256 + at] = 1.0
+                pick[at, second * WIN + other] = 1.0
+                pick[256 + at, other * WIN + second] = 1.0
+    return onehot, place, pick
+
+
+def fused(
+    inputs,
+    target,
+    valid,
+    first_gain,
+    first_shift,
+    triple_weight,
+    query_value_bias,
+    output_weight,
+    output_bias,
+    second_gain,
+    second_shift,
+    expand_weight,
+    expand_bias,
+    shrink_weight,
+    shrink_bias,
+    rows_table,
+    columns_table,
+):
+    onehot, place, pick = constant_tables()
+    vectors = jnp.stack(
+        [
+            first_gain,
+            first_shift,
+            output_bias,
+            second_gain,
+            second_shift,
+            shrink_bias,
+            first_gain,
+            first_gain,
+        ]
+    )
+    q_bias, v_bias = query_value_bias[0], query_value_bias[1]
+    none = jnp.zeros((128,), F32)
+    bias_row = jnp.concatenate(
+        [q_bias[:128], none, v_bias[:128], q_bias[128:], none[:64], v_bias[128:], none[:64], none]
+    )
+    side = jnp.concatenate([jnp.stack([expand_bias, bias_row]), jnp.zeros((6, D), F32)])
+    out_t = output_weight.T
+    q_w, k_w, v_w = triple_weight[0], triple_weight[1], triple_weight[2]
+    attention = jnp.concatenate(
+        [
+            q_w[:, :128],
+            k_w[:, :128],
+            v_w[:, :128],
+            q_w[:, 128:],
+            k_w[:, 128:],
+            v_w[:, 128:],
+            out_t[:, 128:],
+            out_t[:, :128],
+        ],
+        axis=1,
+    )
+    table = jnp.concatenate([rows_table, columns_table, jnp.zeros((10, HEAD), F32)]).astype(BF16)
+    blank = jnp.zeros_like(table)
+    tables = jnp.stack(
+        [jnp.concatenate([table, blank], axis=1), jnp.concatenate([blank, table], axis=1)]
+    )
+    vmem = pl.BlockSpec(memory_space=pltpu.VMEM)
+    big = jax.ShapeDtypeStruct((4, ROWS, D), BF16)
+    part = jax.ShapeDtypeStruct((96, D), F32)
+    copies = 224
+    block, grad, ga, ge, gs, small, table_grad = pl.pallas_call(
+        block_kernel,
+        out_shape=[
+            big,
+            big,
+            part,
+            part,
+            part,
+            jax.ShapeDtypeStruct((16, D), F32),
+            jax.ShapeDtypeStruct((64, 64), F32),
+        ],
+        in_specs=[vmem] * 12,
+        out_specs=[vmem] * 7,
+        scratch_shapes=[
+            pltpu.VMEM((2, 8, 96, D), BF16),
+            pltpu.VMEM((2, 8, 96, D), BF16),
+            pltpu.VMEM((2, 8, 96, D), BF16),
+            pltpu.VMEM((2, 8, D), F32),
+            pltpu.VMEM((2, ROWS, D), F32),
+            pltpu.VMEM((ROWS, D), F32),
+            pltpu.VMEM((ROWS, D), F32),
+            pltpu.VMEM((ROWS, 1), F32),
+            pltpu.VMEM((ROWS, 1), F32),
+            pltpu.VMEM((ROWS, D), F32),
+            pltpu.VMEM((ROWS, D), F32),
+            pltpu.VMEM((2, 2, ROWS, D), BF16),
+            pltpu.VMEM((2, 2, ROWS, D), BF16),
+            pltpu.VMEM((2, 2, ROWS, D), BF16),
+            pltpu.VMEM((2, 2, ROWS, D), BF16),
+            pltpu.VMEM((2, 2, KEYS, 896), BF16),
+            pltpu.VMEM((2, 2, 3, ROWS, KEYS), F32),
+            pltpu.VMEM((2, 2, ROWS, 256), BF16),
+            pltpu.VMEM((2, ROWS, 256), BF16),
+            pltpu.VMEM((2, 2, ROWS, D), BF16),
+            pltpu.VMEM((2, ROWS, D), BF16),
+            pltpu.VMEM((2, 2, ROWS, D), F32),
+            pltpu.VMEM((2, 2, ROWS, D), BF16),
+            pltpu.VMEM((2, ROWS, D), BF16),
+            pltpu.VMEM((2, 2, ROWS, 256), BF16),
+            pltpu.VMEM((2, 2, ROWS, 640), BF16),
+            pltpu.VMEM((2, ROWS, 640), BF16),
+            pltpu.VMEM((2, 512, 128), BF16),
+            pltpu.VMEM((128, 512), F32),
+            pltpu.VMEM((4, ROWS, D), BF16),
+            pltpu.VMEM((4, ROWS, D), BF16),
+            pltpu.VMEM((3, 8, 96, D), F32),
+            pltpu.VMEM((3, 4, 96, D), BF16),
+            pltpu.VMEM((3, 4, 96, D), BF16),
+            pltpu.VMEM((3, 3, 96, D), BF16),
+            pltpu.VMEM((3, 3, 96, D), BF16),
+            pltpu.VMEM((8, 128), F32),
+            pltpu.VMEM((2, 8, 128), F32),
+            pltpu.VMEM((4, 8, 128), F32),
+            pltpu.VMEM((4, 16, D), F32),
+            pltpu.VMEM((6, 16, D), F32),
+            pltpu.VMEM((4, 64, 64), F32),
+            pltpu.VMEM((6, 64, 64), F32),
+            pltpu.SemaphoreType.DMA((copies,)),
+            pltpu.SemaphoreType.DMA((copies,)),
+        ],
+        compiler_params=pltpu.CompilerParams(
+            collective_id=0, has_side_effects=True, vmem_limit_bytes=60 << 20
+        ),
+    )(
+        inputs,
+        target,
+        valid,
+        vectors,
+        side,
+        attention,
+        expand_weight,
+        shrink_weight.T,
+        tables,
+        jnp.asarray(onehot, BF16),
+        jnp.asarray(place, F32),
+        jnp.asarray(pick, BF16),
+    )
+    triple_grad = jnp.stack(
+        [
+            jnp.concatenate([ga[:, 0:128], ga[:, 384:448]], axis=1),
+            jnp.concatenate([ga[:, 128:256], ga[:, 448:512]], axis=1),
+            jnp.concatenate([ga[:, 256:384], ga[:, 512:576]], axis=1),
+        ]
+    )
+    output_grad = jnp.concatenate([ga[:, 640:768], ga[:, 576:640]], axis=1).T
+    bias_grad = small[9]
+    query_value_grad = jnp.stack(
+        [
+            jnp.concatenate([bias_grad[0:128], bias_grad[384:448]]),
+            jnp.concatenate([bias_grad[256:384], bias_grad[512:576]]),
+        ]
+    )
+    return (
+        block[:, :WIN_TOK],
+        small[6, 0],
+        grad[:, :WIN_TOK].astype(F32),
+        small[4],
+        small[5],
+        triple_grad,
+        query_value_grad,
+        output_grad,
+        small[3],
+        small[1],
+        small[2],
+        ge,
+        small[8],
+        gs.T,
+        small[0],
+        table_grad[0:27],
+        table_grad[27:54],
+    )
+
+
 def solution(mesh):
     placed = (
         P("dp", None, None),
@@ -392,8 +1185,9 @@
         P(),
         P(),
     )
+    on_slice = mesh.shape["dp"] == 8 and mesh.shape["tensor"] == 4
     return jax.shard_map(
-        shards,
+        fused if on_slice else shards,
         mesh=mesh,
         in_specs=placed,
         out_specs=(

time: 738 us -> 175 us (0.24)
  waiting for transfers between devices: 247 us -> 0 us
  Pallas kernels: 0 us -> 153 us
  blocking collectives: 140 us -> 0 us
  local copies, waits for them, and re-layouts: 154 us -> 18 us
  matrix products: 88.9 us -> 0 us
  other arithmetic: 79.9 us -> 2.92 us
  between operations: 21.5 us -> 1.03 us
    pallas_call x0 -> x1, Pallas kernels: none -> 153 us  [fused(): pl.pallas_call(block_kernel, out_shape=[big, big, part, part, part, jax.S...]
    psum x4 -> x0, waiting for transfers between devices: 130 us -> none  [row_total(): return lax.psum(partial_value, 'tensor')]
    reduce_scatter x2 -> x0, waiting for transfers between devices: 104 us -> none  [the longest x1 72.3 us: shards(): lax.psum_scatter(shrink_acc, 'dp', scatter_dimension=1, tiled=True)]
    dot_general x50 -> x0, matrix products: 87.6 us -> none  [the longest x2 14.7 us: score_block(): jnp.einsum('gabnc,gefnc->gnabef', queries, keys, preferred_element_type=j...]
    all_gather x2 -> x0, blocking collectives: 70.3 us -> none  [the longest x1 39.1 us: shards(): lax.all_gather(triple_weight, 'dp', axis=1, tiled=True)]
    psum x3 -> x0, blocking collectives: 69.4 us -> none  [the longest x2 58.7 us: shards(): loss_total, count = lax.psum((local_loss, jnp.sum(live)), 'dp')]
    reduce_sum x24 -> x0, other arithmetic: 57.3 us -> none  [the longest x2 15.1 us: shards(): row_part = jnp.sum(grad_grid, axis=5)]
    reshape x18 -> x0, local copies, waits for them, and re-layouts: 52.1 us -> none  [the longest x4 19.4 us: shards(): grad_scores.astype(jnp.float32)]
  transfers between devices with their start and end apart: 10 -> 0, of which waited for: 7 -> 0; matrix products, arithmetic and copies ran while one was open for 23% -> 0% of each run, Pallas kernels for 0% -> 0%
where the time goes in v2:
time: 175 us
  Pallas kernels  153 us (87%)
  local copies, waits for them, and re-layouts  18 us (10%)
  other arithmetic  2.92 us (2%)
    pallas_call x1, Pallas kernels, fused(): pl.pallas_call(block_kernel, out_shape=[big, big, part, part, part, jax.S...  153 us
    unnamed x44, local copies, waits for them, and re-layouts  9.88 us

profile of v2, /device:TPU:0, one launch (start us, length us, event | category | flops | bytes accessed | tf_op | source)
XLA Modules:
  0.0 174.9 jit_solution(12360270121946859980)
XLA Ops:
  0.7 2.5 %copy.38.x_in = bf16[4,196,768]{2,1,0:T(8,128)(2,1)} copy(bf16[4,196,768]{2,0,1:T(4,128)(2,1)} %param.20) | data formatting | bytes 2408448 | tf_op args[0]
  3.3 1.2 copy.39.target_in
  4.6 0.7 stack.65.vectors
  5.4 0.7 maximum_maximum_fusion.side_in
  6.2 0.1 copy.37
  6.4 0.8 concatenate.39.wa_in
  7.3 0.1 pad_bitcast_fusion.1
  7.4 0.6 pad_maximum_fusion.1.tables_in
  8.0 152.9 %shard_map.323 = (bf16[4,208,768]{2,1,0:T(8,128)(2,1)}, bf16[4,208,768]{2,1,0:T(8,128)(2,1)}, f32[96,768]{1,0:T(8,128)}, f32[96,768]{1,0:T(8,128)}, f32[96,768]{...) custom-call(bf16[4,196,768]{2,1,0:T(8,128)(2,1)} %copy.38.x_in, bf16[4,196,768]{2,1,0:T(8,128)(2,1)} %copy.39.target_in, ...), custom_call_target="tpu_custom_call" | custom-call | tf_op jit(solution)/shard_map/pallas_call | solution.py:1055
  161.0 1.4 slice.171
  162.4 1.5 copy.40
  163.9 1.2 slice.172
  165.1 0.2 slice_convert_fusion
  165.2 2.4 %copy.41 = f32[4,196,768]{2,0,1:T(4,128)} copy(f32[4,196,768]{2,1,0:T(8,128)S(1)} %slice_convert_fusion) | data formatting | bytes 4816896
  167.6 1.6 slice_reduce_fusion
  169.2 0.1 fusion.1
  169.4 0.7 pad_maximum_fusion
  170.1 0.7 slice_bitcast_fusion.5
  170.8 0.7 slice_bitcast_fusion.6
  171.5 0.6 pad_maximum_fusion.2
  172.1 0.7 copy.42
  172.8 0.6 fusion.2
  173.5 0.7 copy.45
  174.2 0.7 copy.46
  (70 shorter events, 0.6 us)
Async XLA Ops:
  0.7 2.5 %copy-start = (bf16[4,196,768]{2,0,1:T(4,128)(2,1)S(1)}, bf16[4,196,768]{2,0,1:T(4,128)(2,1)}, u32[]{:S(2)}) copy-start(bf16[4,196,768]{2,0,1:T(4,128)(2,1)} %param.21) | copy-start | bytes 3612676
  3.2 1.3 copy-start.10
  3.2 1.3 copy-start.11
  3.2 1.3 copy-start.12
  3.2 1.3 copy-start.13
  3.2 1.3 copy-start.14
  3.2 1.3 copy-start.15
  3.2 2.0 %copy-start.17 = (f32[2,192]{1,0:T(2,128)S(1)}, f32[2,192]{1,0:T(2,128)}, u32[]{:S(2)}) copy-start(f32[2,192]{1,0:T(2,128)} %param.26) | copy-start | bytes 4612
  3.3 2.1 %copy-start.16 = (f32[768]{0:T(1024)S(1)}, f32[768]{0:T(1024)}, u32[]{:S(2)}) copy-start(f32[768]{0:T(1024)} %param.32) | copy-start | bytes 9220
  3.3 2.9 %copy-start.5 = (bf16[3,96,192]{2,1,0:T(8,128)(2,1)S(1)}, bf16[3,96,192]{2,1,0:T(8,128)(2,1)}, u32[]{:S(2)}) copy-start(bf16[3,96,192]{2,1,0:T(8,128)(2,1)} %param.25) | copy-start | bytes 331780
  3.3 2.9 %copy-start.6 = (bf16[192,96]{1,0:T(8,128)(2,1)S(1)}, bf16[192,96]{1,0:T(8,128)(2,1)}, u32[]{:S(2)}) copy-start(bf16[192,96]{1,0:T(8,128)(2,1)} %param.27) | copy-start | bytes 110596
  4.5 2.7 %copy-start.8 = (f32[27,64]{1,0:T(8,128)S(1)}, f32[27,64]{1,0:T(8,128)}, u32[]{:S(2)}) copy-start(f32[27,64]{1,0:T(8,128)} %param.36) | copy-start | bytes 20740
  4.5 2.7 %copy-start.9 = (f32[27,64]{1,0:T(8,128)S(1)}, f32[27,64]{1,0:T(8,128)}, u32[]{:S(2)}) copy-start(f32[27,64]{1,0:T(8,128)} %param.35) | copy-start | bytes 20740
  162.4 2.7 %copy-start.1 = (bf16[4,208,768]{2,1,0:T(8,128)(2,1)S(1)}, bf16[4,208,768]{2,1,0:T(8,128)(2,1)}, u32[]{:S(2)}) copy-start(bf16[4,208,768]{2,1,0:T(8,128)(2,1)} %get-tuple-element.26) | copy-start | bytes 3833860
  165.2 4.0 %copy-start.2 = (f32[96,768]{1,0:T(8,128)S(1)}, f32[96,768]{1,0:T(8,128)}, u32[]{:S(2)}) copy-start(f32[96,768]{1,0:T(8,128)} %get-tuple-element.27) | copy-start | bytes 884740
  167.6 5.3 %copy-start.7 = (f32[64,64]{1,0:T(8,128)S(1)}, f32[64,64]{1,0:T(8,128)}, u32[]{:S(2)}) copy-start(f32[64,64]{1,0:T(8,128)} %get-tuple-element.30) | copy-start | bytes 49156
  169.2 4.2 %copy-start.4 = (f32[96,768]{1,0:T(8,128)S(1)}, f32[96,768]{1,0:T(8,128)}, u32[]{:S(2)}) copy-start(f32[96,768]{1,0:T(8,128)} %get-tuple-element.110) | copy-start | bytes 884740
  169.3 4.9 %copy-start.3 = (f32[96,768]{1,0:T(8,128)S(1)}, f32[96,768]{1,0:T(8,128)}, u32[]{:S(2)}) copy-start(f32[96,768]{1,0:T(8,128)} %get-tuple-element.29) | copy-start | bytes 884740

commit v3 on v2

--- a/solution.py
+++ b/solution.py
@@ -417,15 +417,23 @@
     x_in,
     target_in,
     valid_in,
-    vectors,
-    side_in,
-    wa_in,
+    gain1_in,
+    shift1_in,
+    triple_in,
+    qv_bias_in,
+    out_w_in,
+    bias_out_in,
+    gain2_in,
+    shift2_in,
     we_in,
+    expand_bias_in,
     ws_in,
-    tables_in,
-    onehot,
-    place,
-    pick,
+    bias_shrink_in,
+    rows_in,
+    columns_in,
+    onehot_in,
+    place_in,
+    pick_in,
     block_out,
     grad_out,
     ga_out,
@@ -433,9 +441,23 @@
     gs_out,
     small_out,
     table_out,
+    wa_in,
     wa,
     we,
     ws,
+    xt,
+    tt,
+    onehot,
+    place,
+    pick,
+    tabs,
+    bo,
+    ig,
+    mix,
+    bo_low,
+    ga,
+    ge,
+    gs,
     side,
     xf,
     unit1,
@@ -469,13 +491,13 @@
     xr,
     zs,
     zr,
-    ig,
     cnt,
     cntr,
     sb,
     sbr,
     tb,
     tbr,
+    load_sem,
     send_sem,
     recv_sem,
 ):
@@ -508,6 +530,19 @@
         started.append(copy)
         return copy
 
+    loads = []
+
+    def load(src, dst):
+        copy = pltpu.make_async_copy(src, dst, load_sem.at[len(loads)])
+        copy.start()
+        loads.append(copy)
+        return copy
+
+    x_load = load(x_in, xt)
+    onehot_load = load(onehot_in, onehot)
+    place_load = load(place_in, place)
+    pick_load = load(pick_in, pick)
+    target_load = load(target_in, tt)
     barrier = pltpu.get_barrier_semaphore()
     for mate in z_mates + [x_mate, y_mate, c_mate]:
         pl.semaphore_signal(barrier, inc=1, device_id=mate, device_id_type=MESH)
@@ -545,19 +580,45 @@
         for k in range(8):
             from_c[g, k].wait_recv()
 
+    for i in range(3):
+        wa_in[:, 128 * i : 128 * i + 128] = triple_in[i, :, 0:128]
+    source = lax.broadcasted_iota(jnp.int32, (192, 256), 0)
+    column = lax.broadcasted_iota(jnp.int32, (192, 256), 1)
+    tail = sum(
+        dot_nn(
+            triple_in[i],
+            ((source >= 128) & (source - 128 == column - 64 * i)).astype(F32).astype(BF16),
+        )
+        for i in range(3)
+    )
+    out_w = out_w_in[...]
+    tail = tail + dot_tn(
+        out_w, ((source >= 128) & (source + 64 == column)).astype(F32).astype(BF16)
+    )
+    wa_in[:, 384:640] = tail.astype(BF16)
+    wa_in[:, 640:768] = dot_tn(
+        out_w, (source == column).astype(F32).astype(BF16)[:, 0:128]
+    ).astype(BF16)
     gather_start(0)
-    side_copy = send(side_in, side.at[1], c_mate)
-    side[0] = side_in[...]
+    gather_start(1)
+    gather_start(2)
+    side[0] = jnp.zeros((8, D), F32)
+    side[0, 0:1, :] = expand_bias_in[...].reshape(1, D)
+    side[0, 1:2, 0:128] = qv_bias_in[0:1, 0:128]
+    side[0, 1:2, 256:384] = qv_bias_in[1:2, 0:128]
+    side[0, 1:2, 384:448] = qv_bias_in[0:1, 128:192]
+    side[0, 1:2, 512:576] = qv_bias_in[1:2, 128:192]
+    side_copy = send(side.at[0], side.at[1], c_mate)
     marks_all = valid_in[...].astype(F32)
     cnt[0] = jnp.full((8, 128), jnp.sum(marks_all), F32)
     cnt_x = send(cnt.at[0], cntr.at[0], x_mate)
 
-    gain1 = vectors[0:1, :]
-    shift1 = vectors[1:2, :]
-    bias_out = vectors[2:3, :]
-    gain2 = vectors[3:4, :]
-    shift2 = vectors[4:5, :]
-    bias_shrink = vectors[5:6, :]
+    gain1 = gain1_in[...].reshape(1, D)
+    shift1 = shift1_in[...].reshape(1, D)
+    bias_out = bias_out_in[...].reshape(1, D)
+    gain2 = gain2_in[...].reshape(1, D)
+    shift2 = shift2_in[...].reshape(1, D)
+    bias_shrink = bias_shrink_in[...].reshape(1, D)
 
     lane = lax.broadcasted_iota(jnp.int32, (1, 128), 1)
     half = ((lane < 64).astype(F32), (lane >= 64).astype(F32))
@@ -573,9 +634,15 @@
     )
     live = jnp.sum(jnp.where(eye, own_marks, 0.0), axis=1, keepdims=True)
 
+    window_ids = lax.broadcasted_iota(jnp.int32, (1, 4, 1), 1)
+
+    def window_of(ref, window):
+        return jnp.sum(ref[...].astype(F32) * (window_ids == window).astype(F32), axis=1)
+
     xf[...] = jnp.zeros_like(xf)
-    xf[0, 0:WIN_TOK, :] = x_in[t].astype(F32)
-    xf[1, 0:WIN_TOK, :] = x_in[peer_window].astype(F32)
+    x_load.wait()
+    xf[0, 0:WIN_TOK, :] = window_of(xt, t)
+    xf[1, 0:WIN_TOK, :] = window_of(xt, peer_window)
     for w in range(2):
         unit, inverse = normalize(xf[w])
         n1[0, w] = (unit * gain1 + shift1).astype(BF16)
@@ -583,14 +650,19 @@
             unit1[...] = unit
             inv1[...] = inverse
     n1_copy = send(n1.at[0], n1.at[1], c_mate)
-    for p in range(2):
-        t2[p] = dot_nn(onehot[...], tables_in[p]).astype(BF16)
+    tabs[...] = jnp.zeros_like(tabs)
+    tabs[0:27, 0:64] = rows_in[...]
+    tabs[32:59, 0:64] = columns_in[...]
+    onehot_load.wait()
+    t2[0] = dot_nn(onehot[...], tabs[...].astype(BF16)).astype(BF16)
+    t2[1] = dot_nn(onehot[...], pltpu.roll(tabs[...], 64, 1).astype(BF16)).astype(BF16)
+    place_load.wait()
+    pick_load.wait()
     pj[:, :, ROWS:, :] = jnp.zeros((2, 2, KEYS - ROWS, 896), BF16)
     tg[...] = jnp.zeros_like(tg)
 
     for k in (1, 2, 3):
         gather_z(0, k)
-    gather_start(1)
     for k in range(4):
         gather_x(0, k)
     cnt_x.wait_recv()
@@ -651,7 +723,6 @@
         e1.append(send(es.at[0, pl.ds(lo, n)], er.at[0, pl.ds(lo, n)], y_mate))
     for k in (1, 2, 3):
         gather_z(1, k)
-    gather_start(2)
     project(0)
     for k in range(4):
         gather_x(1, k)
@@ -713,7 +784,8 @@
     count = (cnt[1] + cntr[1]) + (cntr[2] + cntr[3])
     count = count[0:1, 0:1]
     scaled_live = live * (token_total / count)
-    xf[1, 0:WIN_TOK, :] = target_in[t].astype(F32)
+    target_load.wait()
+    xf[1, 0:WIN_TOK, :] = window_of(tt, t)
     xf[1, WIN_TOK:, :] = jnp.zeros((ROWS - WIN_TOK, D), F32)
     e4 = []
     gr_c = []
@@ -729,7 +801,7 @@
         gr[0, 0, lo : lo + n, :] = grad.astype(BF16)
         e4.append(send(gr.at[0, 0, rows], gr.at[0, 1, rows], y_mate))
         gr_c.append(send(gr.at[0, 0, rows], gr.at[1, 0, rows], c_mate))
-        block_out[t, lo : lo + n, :] = result.astype(BF16)
+        bo[t, lo : lo + n, :] = result.astype(BF16)
         loss_part = loss_part + column_sum(gap * gap * live[lo : lo + n, :])
         shrink_bias_part = shrink_bias_part + column_sum(grad)
     sb[0] = jnp.zeros((16, D), F32)
@@ -822,8 +894,8 @@
     sb[0, 2:3, :] = shift_part
     sb[0, 3:4, :] = bias_part
 
-    bo_y = send(block_out.at[t], block_out.at[t], y_mate)
-    bo_c = [send(block_out.at[t], block_out.at[t], c_mate)]
+    bo_y = send(bo.at[t], bo.at[t], y_mate)
+    bo_c = [send(bo.at[t], bo.at[t], c_mate)]
     gb_copy.wait_recv()
     for copy in n2_c:
         copy.wait_recv()
@@ -915,12 +987,13 @@
         gain_part = gain_part + column_sum(grad * unit)
         shift_part = shift_part + column_sum(grad)
         grad = acc[lo : lo + n, :] + normalize_back(grad, unit, inv1[lo : lo + n, :], gain1)
-        grad_out[t, lo : lo + n, :] = grad.astype(BF16)
-        e8.append(send(grad_out.at[t, rows], grad_out.at[t, rows], y_mate))
-        ig_c.append(send(grad_out.at[t, rows], grad_out.at[t, rows], c_mate))
+        ig[t, lo : lo + n, :] = grad.astype(BF16)
+        e8.append(send(ig.at[t, rows], ig.at[t, rows], y_mate))
+        ig_c.append(send(ig.at[t, rows], ig.at[t, rows], c_mate))
     sb[0, 4:5, :] = gain_part
     sb[0, 5:6, :] = shift_part
 
+    scatter_z(0)
     spread = tg[...]
     spread_high = spread.astype(BF16)
     spread_low = (spread - spread_high.astype(F32)).astype(BF16)
@@ -942,7 +1015,6 @@
     tb[2] = tb[1] + tbr[1]
     s_x = send(sb.at[2], sbr.at[2], x_mate)
     t_x = send(tb.at[2], tbr.at[2], x_mate)
-    scatter_z(0)
     s_x.wait_recv()
     t_x.wait_recv()
     sb[3] = sb[2] + sbr[2]
@@ -951,14 +1023,28 @@
     t_z = [send(tb.at[3], tbr.at[2 + k], z_mates[k - 1]) for k in (1, 2, 3)]
 
     bo_y.wait_recv()
-    bo_c.append(send(block_out.at[peer_window], block_out.at[peer_window], c_mate))
+    bo_c.append(send(bo.at[peer_window], bo.at[peer_window], c_mate))
+    scatter_end(2, gs)
+    gs_store = load(gs, gs_out)
+    scatter_end(1, ge)
+    ge_store = load(ge, ge_out)
+    for copy in bo_c:
+        copy.wait_recv()
+    for w in range(4):
+        mix[:, w, :] = bo[w, 0:WIN_TOK, :].astype(F32)
+    bo_low[...] = mix[...].astype(BF16)
+    bo_store = load(bo_low, block_out)
     for i, (lo, n) in enumerate(CHUNKS):
         rows = pl.ds(lo, n)
         e8[i].wait_recv()
-        ig_c.append(send(grad_out.at[peer_window, rows], grad_out.at[peer_window, rows], c_mate))
-    scatter_end(2, gs_out)
-    scatter_end(1, ge_out)
-    scatter_end(0, ga_out)
+        ig_c.append(send(ig.at[peer_window, rows], ig.at[peer_window, rows], c_mate))
+    for copy in ig_c:
+        copy.wait_recv()
+    for w in range(4):
+        mix[:, w, :] = ig[w, 0:WIN_TOK, :].astype(F32)
+    ig_store = load(mix, grad_out)
+    scatter_end(0, ga)
+    ga_store = load(ga, ga_out)
     for copy in s_z + t_z:
         copy.wait_recv()
     total = (sb[3] + sbr[3]) + (sbr[4] + sbr[5])
@@ -967,10 +1053,82 @@
         jnp.sum(total[6:7, :], axis=1, keepdims=True) / (count * float(D)), (1, D)
     )
     table_out[...] = ((tb[3] + tbr[3]) + (tbr[4] + tbr[5])).T
-    for copy in bo_c + ig_c:
-        copy.wait_recv()
     for copy in started:
         copy.wait_send()
+    for copy in (gs_store, ge_store, bo_store, ig_store, ga_store):
+        copy.wait()
+
+
+def finish_kernel(
+    block_in,
+    grad_in,
+    ga,
+    ge,
+    gs,
+    small,
+    table,
+    block_out,
+    loss_out,
+    grad_out,
+    gain1_out,
+    shift1_out,
+    triple_out,
+    qv_out,
+    out_w_out,
+    out_b_out,
+    gain2_out,
+    shift2_out,
+    we_out,
+    expand_bias_out,
+    ws_out,
+    bias_shrink_out,
+    rows_out,
+    columns_out,
+    block_hold,
+    grad_hold,
+    ge_hold,
+    gs_hold,
+    sems,
+):
+    moves = []
+    at = 0
+    for src, hold, dst, step in (
+        (block_in, block_hold, block_out, 49),
+        (grad_in, grad_hold, grad_out, 49),
+        (ge, ge_hold, we_out, 96),
+        (gs, gs_hold, ws_out, 96),
+    ):
+        for lo in range(0, src.shape[0], step):
+            rows = pl.ds(lo, step)
+            copy = pltpu.make_async_copy(src.at[rows], hold.at[rows], sems.at[at])
+            copy.start()
+            moves.append(
+                (copy, pltpu.make_async_copy(hold.at[rows], dst.at[rows], sems.at[at + 1]))
+            )
+            at += 2
+    for i in range(3):
+        triple_out[i, :, 0:128] = ga[:, 128 * i : 128 * i + 128]
+    triple_out[0, :, 128:192] = ga[:, 384:448]
+    triple_out[1, :, 128:192] = pltpu.roll(ga[:, 384:512], 64, 1)[:, 0:64]
+    triple_out[2, :, 128:192] = ga[:, 512:576]
+    out_w_out[0:128, :] = ga[:, 640:768].T
+    out_w_out[128:192, :] = ga[:, 512:640].T[64:128]
+    loss_out[...] = small[6:7, 0:1]
+    for i, out in enumerate(
+        (bias_shrink_out, gain2_out, shift2_out, out_b_out, gain1_out, shift1_out)
+    ):
+        out[...] = small[i]
+    expand_bias_out[...] = small[8]
+    for i in range(2):
+        qv_out[i : i + 1, 0:128] = small[9:10, 256 * i : 256 * i + 128]
+        qv_out[i : i + 1, 128:192] = small[9:10, 384 + 128 * i : 448 + 128 * i]
+    rows_out[...] = table[0:27]
+    columns_out[...] = table[32:59]
+    for arrive, leave in moves:
+        arrive.wait()
+        leave.start()
+    for arrive, leave in moves:
+        leave.wait()
 
 
 def constant_tables():
@@ -981,7 +1139,7 @@
         for second in range(WIN):
             at = first * WIN + second
             onehot[at, first - second + WIN - 1] = 1.0
-            onehot[256 + at, 27 + first - second + WIN - 1] = 1.0
+            onehot[256 + at, 32 + first - second + WIN - 1] = 1.0
             for other in range(WIN):
                 place[first * WIN + other, at] = 1.0
                 place[other * WIN + first, 256 + at] = 1.0
@@ -1010,65 +1168,42 @@
     columns_table,
 ):
     onehot, place, pick = constant_tables()
-    vectors = jnp.stack(
-        [
-            first_gain,
-            first_shift,
-            output_bias,
-            second_gain,
-            second_shift,
-            shrink_bias,
-            first_gain,
-            first_gain,
-        ]
-    )
-    q_bias, v_bias = query_value_bias[0], query_value_bias[1]
-    none = jnp.zeros((128,), F32)
-    bias_row = jnp.concatenate(
-        [q_bias[:128], none, v_bias[:128], q_bias[128:], none[:64], v_bias[128:], none[:64], none]
-    )
-    side = jnp.concatenate([jnp.stack([expand_bias, bias_row]), jnp.zeros((6, D), F32)])
-    out_t = output_weight.T
-    q_w, k_w, v_w = triple_weight[0], triple_weight[1], triple_weight[2]
-    attention = jnp.concatenate(
-        [
-            q_w[:, :128],
-            k_w[:, :128],
-            v_w[:, :128],
-            q_w[:, 128:],
-            k_w[:, 128:],
-            v_w[:, 128:],
-            out_t[:, 128:],
-            out_t[:, :128],
-        ],
-        axis=1,
-    )
-    table = jnp.concatenate([rows_table, columns_table, jnp.zeros((10, HEAD), F32)]).astype(BF16)
-    blank = jnp.zeros_like(table)
-    tables = jnp.stack(
-        [jnp.concatenate([table, blank], axis=1), jnp.concatenate([blank, table], axis=1)]
-    )
     vmem = pl.BlockSpec(memory_space=pltpu.VMEM)
-    big = jax.ShapeDtypeStruct((4, ROWS, D), BF16)
+    anywhere = pl.BlockSpec(memory_space=pl.ANY)
+    mixed_shape = (WIN_TOK, 4, D)
     part = jax.ShapeDtypeStruct((96, D), F32)
     copies = 224
-    block, grad, ga, ge, gs, small, table_grad = pl.pallas_call(
+    parts = pl.pallas_call(
         block_kernel,
         out_shape=[
-            big,
-            big,
+            jax.ShapeDtypeStruct(mixed_shape, BF16),
+            jax.ShapeDtypeStruct(mixed_shape, F32),
             part,
             part,
             part,
             jax.ShapeDtypeStruct((16, D), F32),
             jax.ShapeDtypeStruct((64, 64), F32),
         ],
-        in_specs=[vmem] * 12,
-        out_specs=[vmem] * 7,
+        in_specs=[anywhere] * 2 + [vmem] * 15 + [anywhere] * 3,
+        out_specs=[anywhere] * 5 + [vmem] * 2,
         scratch_shapes=[
+            pltpu.VMEM((96, D), BF16),
             pltpu.VMEM((2, 8, 96, D), BF16),
             pltpu.VMEM((2, 8, 96, D), BF16),
             pltpu.VMEM((2, 8, 96, D), BF16),
+            pltpu.VMEM(mixed_shape, BF16),
+            pltpu.VMEM(mixed_shape, BF16),
+            pltpu.VMEM((512, 64), BF16),
+            pltpu.VMEM((ROWS, 512), F32),
+            pltpu.VMEM((512, KEYS), BF16),
+            pltpu.VMEM((64, 128), F32),
+            pltpu.VMEM((4, ROWS, D), BF16),
+            pltpu.VMEM((4, ROWS, D), BF16),
+            pltpu.VMEM(mixed_shape, F32),
+            pltpu.VMEM(mixed_shape, BF16),
+            pltpu.VMEM((96, D), F32),
+            pltpu.VMEM((96, D), F32),
+            pltpu.VMEM((96, D), F32),
             pltpu.VMEM((2, 8, D), F32),
             pltpu.VMEM((2, ROWS, D), F32),
             pltpu.VMEM((ROWS, D), F32),
@@ -1102,13 +1237,13 @@
             pltpu.VMEM((3, 4, 96, D), BF16),
             pltpu.VMEM((3, 3, 96, D), BF16),
             pltpu.VMEM((3, 3, 96, D), BF16),
-            pltpu.VMEM((8, 128), F32),
             pltpu.VMEM((2, 8, 128), F32),
             pltpu.VMEM((4, 8, 128), F32),
             pltpu.VMEM((4, 16, D), F32),
             pltpu.VMEM((6, 16, D), F32),
             pltpu.VMEM((4, 64, 64), F32),
             pltpu.VMEM((6, 64, 64), F32),
+            pltpu.SemaphoreType.DMA((16,)),
             pltpu.SemaphoreType.DMA((copies,)),
             pltpu.SemaphoreType.DMA((copies,)),
         ],
@@ -1116,53 +1251,68 @@
             collective_id=0, has_side_effects=True, vmem_limit_bytes=60 << 20
         ),
     )(
-        inputs,
-        target,
+        inputs.transpose(1, 0, 2),
+        target.transpose(1, 0, 2),
         valid,
-        vectors,
-        side,
-        attention,
+        first_gain,
+        first_shift,
+        triple_weight,
+        query_value_bias,
+        output_weight,
+        output_bias,
+        second_gain,
+        second_shift,
         expand_weight,
+        expand_bias,
         shrink_weight.T,
-        tables,
+        shrink_bias,
+        rows_table,
+        columns_table,
         jnp.asarray(onehot, BF16),
         jnp.asarray(place, F32),
         jnp.asarray(pick, BF16),
     )
-    triple_grad = jnp.stack(
-        [
-            jnp.concatenate([ga[:, 0:128], ga[:, 384:448]], axis=1),
-            jnp.concatenate([ga[:, 128:256], ga[:, 448:512]], axis=1),
-            jnp.concatenate([ga[:, 256:384], ga[:, 512:576]], axis=1),
-        ]
-    )
-    output_grad = jnp.concatenate([ga[:, 640:768], ga[:, 576:640]], axis=1).T
-    bias_grad = small[9]
-    query_value_grad = jnp.stack(
-        [
-            jnp.concatenate([bias_grad[0:128], bias_grad[384:448]]),
-            jnp.concatenate([bias_grad[256:384], bias_grad[512:576]]),
-        ]
-    )
-    return (
-        block[:, :WIN_TOK],
-        small[6, 0],
-        grad[:, :WIN_TOK].astype(F32),
-        small[4],
-        small[5],
-        triple_grad,
-        query_value_grad,
-        output_grad,
-        small[3],
-        small[1],
-        small[2],
-        ge,
-        small[8],
-        gs.T,
-        small[0],
-        table_grad[0:27],
-        table_grad[27:54],
-    )
+    vector = jax.ShapeDtypeStruct((D,), F32)
+    relative = jax.ShapeDtypeStruct(rows_table.shape, F32)
+    outs = pl.pallas_call(
+        finish_kernel,
+        out_shape=[
+            jax.ShapeDtypeStruct(mixed_shape, BF16),
+            jax.ShapeDtypeStruct((1, 1), F32),
+            jax.ShapeDtypeStruct(mixed_shape, F32),
+            vector,
+            vector,
+            jax.ShapeDtypeStruct(triple_weight.shape, F32),
+            jax.ShapeDtypeStruct(query_value_bias.shape, F32),
+            jax.ShapeDtypeStruct(output_weight.shape, F32),
+            vector,
+            vector,
+            vector,
+            part,
+            jax.ShapeDtypeStruct(expand_bias.shape, F32),
+            part,
+            vector,
+            relative,
+            relative,
+        ],
+        in_specs=[anywhere] * 2 + [vmem, anywhere, anywhere] + [vmem] * 2,
+        out_specs=[
+            anywhere if i in (0, 2, 11, 13) else vmem for i in range(17)
+        ],
+        scratch_shapes=[
+            pltpu.VMEM(mixed_shape, BF16),
+            pltpu.VMEM(mixed_shape, F32),
+            pltpu.VMEM((96, D), F32),
+            pltpu.VMEM((96, D), F32),
+            pltpu.SemaphoreType.DMA((20,)),
+        ],
+    )(*parts)
+    outs = list(outs)
+    outs[0] = outs[0].transpose(1, 0, 2)
+    outs[1] = outs[1].reshape(())
+    outs[2] = outs[2].transpose(1, 0, 2)
+    outs[13] = outs[13].T
+    return tuple(outs)
 
 
 def solution(mesh):

time: 175 us -> 156 us (0.89)
  local copies, waits for them, and re-layouts: 18 us -> 0 us
  other arithmetic: 2.92 us -> 0 us
  Pallas kernels: 153 us -> 155 us
    unnamed x44 -> x0, local copies, waits for them, and re-layouts: 9.88 us -> none
    slice x18 -> x0, local copies, waits for them, and re-layouts: 6.33 us -> none  [the longest x1 1.63 us: fused(): small[0]]
    another operation x7 -> x0, other arithmetic: 1.98 us -> none  [the longest x3 0.76 us: fused(): jnp.stack([jnp.concatenate([ga[:, 0:128], ga[:, 384:448]], axis=1), jnp.c...]
    pallas_call x1 -> x2, Pallas kernels: 153 us -> 155 us  [the longest x1 149 us: fused(): pl.pallas_call(block_kernel, out_shape=[jax.ShapeDtypeStruct(mixed_shape,...]
where the time goes in v3:
time: 156 us; the launch traced here: 155 us
  Pallas kernels  155 us (99%)
    pallas_call x1, Pallas kernels, fused(): pl.pallas_call(block_kernel, out_shape=[jax.ShapeDtypeStruct(mixed_shape,...  149 us
    pallas_call x1, Pallas kernels, fused(): pl.pallas_call(finish_kernel, out_shape=[jax.ShapeDtypeStruct(mixed_shape...  5.53 us

profile of v3, /device:TPU:0, one launch (start us, length us, event | category | flops | bytes accessed | tf_op | source)
XLA Modules:
  0.0 155.4 jit_solution(877187008139438043)
XLA Ops:
  0.7 149.0 %shard_map.323 = (bf16[196,4,768]{2,1,0:T(4,128)(2,1)}, f32[196,4,768]{2,1,0:T(4,128)}, f32[96,768]{1,0:T(8,128)}, f32[96,768]{1,0:T(8,128)}, f32[96,768]{1,0:T(...) custom-call(bf16[196,4,768]{2,1,0:T(4,128)(2,1)} %bitcast.7, bf16[196,4,768]{2,1,0:T(4,128)(2,1)} %bitcast.8, ...), custom_call_target="tpu_custom_call" | custom-call | tf_op jit(solution)/shard_map/pallas_call | solution.py:1176
  149.7 5.5 %shard_map.324 = (bf16[196,4,768]{2,1,0:T(4,128)(2,1)}, f32[1,1]{1,0:T(1,128)}, f32[196,4,768]{2,1,0:T(4,128)}, f32[768]{0:T(1024)}, f32[768]{0:T(1024)}, /*inde...) custom-call(bf16[196,4,768]{2,1,0:T(4,128)(2,1)} %get-tuple-element., ...), custom_call_target="tpu_custom_call" | custom-call | tf_op jit(solution)/shard_map/pallas_call | solution.py:1277
